TPU v7x, 256 devices: a whole 4x4x8 slice. The times are simulated.
256 devices in a mesh: ctx: 32 (over y, z), tp: 8 (over x, core).
Axes of the slice: x: 4, y: 4, z: 8, core: 2. Of those that a mesh axis runs over, the one named last changes fastest.
Arguments:
- context_queries: bfloat16 [24576, 8192], P('ctx', 'tp'), may hold values from -160 to 160
- context_keys: bfloat16 [24576, 1024], P('ctx', 'tp'), may hold values from -5 to 5
- context_values: bfloat16 [24576, 1024], P('ctx', 'tp'), may hold values from -6 to 6
- block_length: int32 [32], P('ctx'), may hold values from 1 to 768, 18432 in all
- question_queries: bfloat16 [256, 8192], P('ctx', 'tp'), may hold values from -160 to 160
- question_keys: bfloat16 [256, 1024], P('ctx', 'tp'), may hold values from -6 to 6
- question_values: bfloat16 [256, 1024], P('ctx', 'tp'), may hold values from -6 to 6
- query_position: int32 [256], P('ctx'), may hold values from 0 to 255, each once
- out_weight: bfloat16 [8192, 8192], P('tp', 'ctx'), may hold values from -0.0625 to 0.0625
Outputs:
- block_output: bfloat16 [24576, 8192], P('ctx', 'tp')
- answer: bfloat16 [256, 8192], P(None, 'ctx')
Inputs may be any that keep to these rules, and one draw needn't show every extreme that they name: `block_length`: the largest entry equals 768; the entries sum to 18432. `query_position`: A permutation.
All inputs are finite; a program needn't handle non-finite values. No bound on the sum of `block_length` on one device may be relied on, other than what follows from the above.
Results may differ from a plain program's by a relative error of at most 0.008.
Values may be sent and summed in bfloat16 or wider, within the bound.
A program may use at most 192 MiB of HBM per device.

v0:
```python
import math

import jax
import jax.numpy as jnp
from jax import lax
from jax.sharding import PartitionSpec as P

HEAD_SIZE = 128


NEG = -1e30


def broadcast(block, axis, source):
    block = jnp.where(lax.axis_index(axis) == source, block, jnp.zeros_like(block))
    return lax.psum(block, axis)


def softmax_parts(scores, visible):
    masked = jnp.where(visible, scores, NEG)
    highest = jnp.max(masked, axis=-1)
    weights = jnp.where(visible, jnp.exp(masked - highest[..., None]), 0.0)
    total = jnp.sum(weights, axis=-1)
    return (highest, total, weights.astype(jnp.bfloat16))


def encode_head(
    query_matrix,
    key_rows,
    value_rows,
    anchor_keys,
    anchor_values,
    own_length,
    anchor_length,
    uses_anchor,
):
    rows = query_matrix.shape[0]
    row_index = lax.broadcasted_iota(jnp.int32, (rows, rows), 0)
    col_index = lax.broadcasted_iota(jnp.int32, (rows, rows), 1)
    anchor_seen = (col_index < anchor_length) & uses_anchor
    own_seen = (col_index <= row_index) & (col_index < own_length)
    visible = jnp.concatenate([anchor_seen, own_seen], axis=1)
    keys_all = jnp.concatenate([anchor_keys, key_rows], axis=0)
    values_all = jnp.concatenate([anchor_values, value_rows], axis=0)
    scores = jnp.einsum(
        "rgd,kd->grk", query_matrix, keys_all, preferred_element_type=jnp.float32
    ) / math.sqrt(HEAD_SIZE)
    highest, total, rounded = softmax_parts(scores, visible[None])
    summed = jnp.einsum("grk,kd->grd", rounded, values_all, preferred_element_type=jnp.float32)
    return jnp.transpose((summed / total[..., None]).astype(jnp.bfloat16), (1, 0, 2))


def body(
    context_queries,
    context_keys,
    context_values,
    block_length,
    question_queries,
    question_keys,
    question_values,
    query_position,
    out_weight,
):
    rows = context_queries.shape[0]
    kv_local = context_keys.shape[1] // HEAD_SIZE
    heads_local = context_queries.shape[1] // HEAD_SIZE
    head_group = heads_local // kv_local
    place = lax.axis_index("ctx")
    anchor_keys, anchor_values, anchor_length = (
        broadcast(context_keys, "ctx", 0),
        broadcast(context_values, "ctx", 0),
        broadcast(block_length, "ctx", 0),
    )
    gathered_rows, gathered_position = (
        lax.all_gather(question_queries, "ctx", axis=0, tiled=True),
        lax.all_gather(query_position, "ctx", axis=0, tiled=True),
    )
    asked_rows = gathered_rows.reshape(-1, kv_local, head_group, HEAD_SIZE)
    total_rows = asked_rows.shape[0]
    keys_all = jnp.concatenate([context_keys, question_keys], axis=0).reshape(
        -1, kv_local, HEAD_SIZE
    )
    values_all = jnp.concatenate([context_values, question_values], axis=0).reshape(
        -1, kv_local, HEAD_SIZE
    )
    context_seen = jnp.broadcast_to(
        jnp.arange(rows, dtype=jnp.int32)[None, :] < block_length[0], (total_rows, rows)
    )
    query_seen = query_position[None, :] <= gathered_position[:, None]
    visible = jnp.concatenate([context_seen, query_seen], axis=1)
    scores = jnp.einsum(
        "qhgd,khd->hgqk", asked_rows, keys_all, preferred_element_type=jnp.float32
    ) / math.sqrt(HEAD_SIZE)
    highest, total, rounded = softmax_parts(scores, visible[None, None])
    summed = jnp.einsum("hgqk,khd->hgqd", rounded, values_all, preferred_element_type=jnp.float32)
    highest = highest.reshape(heads_local, total_rows)
    total = total.reshape(heads_local, total_rows)
    summed = summed.reshape(heads_local, total_rows, HEAD_SIZE)
    head_queries = jnp.transpose(
        context_queries.reshape(rows, kv_local, head_group, HEAD_SIZE), (1, 0, 2, 3)
    )
    head_keys = jnp.transpose(context_keys.reshape(rows, kv_local, HEAD_SIZE), (1, 0, 2))
    head_values = jnp.transpose(context_values.reshape(rows, kv_local, HEAD_SIZE), (1, 0, 2))
    head_anchor_keys = jnp.transpose(anchor_keys.reshape(rows, kv_local, HEAD_SIZE), (1, 0, 2))
    head_anchor_values = jnp.transpose(anchor_values.reshape(rows, kv_local, HEAD_SIZE), (1, 0, 2))

    def per_head(head_pack):
        head_q, head_k, head_v, head_ak, head_av = head_pack
        return encode_head(
            head_q, head_k, head_v, head_ak, head_av, block_length[0], anchor_length[0], place != 0
        )

    encoded = lax.map(
        per_head, (head_queries, head_keys, head_values, head_anchor_keys, head_anchor_values)
    )
    block_output = jnp.transpose(encoded, (1, 0, 2, 3)).reshape(rows, heads_local * HEAD_SIZE)
    merged_max = lax.pmax(highest, "ctx")
    factor = jnp.exp(highest - merged_max)
    merged_total, merged_sum = lax.psum((total * factor, summed * factor[..., None]), "ctx")
    attention = (merged_sum / merged_total[..., None]).astype(jnp.bfloat16)
    weight = out_weight.reshape(heads_local, HEAD_SIZE, -1)
    partial_answer = jnp.einsum(
        "hqd,hde->qe", attention, weight, preferred_element_type=jnp.float32
    )
    answer = lax.psum(partial_answer, "tp").astype(jnp.bfloat16)
    return (block_output, answer)


def solution(mesh):
    in_specs = (
        P("ctx", "tp"),
        P("ctx", "tp"),
        P("ctx", "tp"),
        P("ctx"),
        P("ctx", "tp"),
        P("ctx", "tp"),
        P("ctx", "tp"),
        P("ctx"),
        P("tp", "ctx"),
    )
    out_specs = (P("ctx", "tp"), P(None, "ctx"))
    return jax.shard_map(body, mesh=mesh, in_specs=in_specs, out_specs=out_specs, check_vma=False)
```

profile of v0, /device:TPU:1, one launch (start us, length us, event | category | flops | bytes accessed | tf_op | source)
XLA Modules:
  0.0 348.6 jit_solution(13577622784609710838)
XLA Ops:
  7.2 0.0 copy-start
  7.2 0.0 all-reduce.9.cloned.1.call-start
  7.2 1.7 broadcast_select_fusion.1
  9.0 1.6 broadcast_select_fusion
  10.6 0.0 all-reduce.9.cloned.1.call-update
  10.6 0.0 all-reduce.7.cloned.1.call-start
  11.3 1.3 dynamic-slice.4
  13.4 0.9 dynamic-update-slice
  14.3 19.6 %all-reduce.1 = (s32[]{:T(128)}, s32[256]{0:T(256)S(1)}) all-reduce(s32[]{:T(128)} %bitcast.1, s32[256]{0:T(256)S(1)} %dynamic-update-slice), channel_id=1, replica_groups=mesh['ctx'=32,'tp'=8] {'ctx'}, use_global_device_ids=true, to_apply=%region_0.1 | all-reduce | flops 257 | bytes 2056 | tf_op jit(solution)/shard_map/psum | solution.py:16
  33.8 0.7 broadcast_compare_fusion
  34.6 36.4 %all_gather.7 = bf16[256,1024]{1,0:T(8,128)(2,1)S(1)} all-gather(bf16[8,1024]{1,0:T(8,128)(2,1)} %param.13), channel_id=1, replica_groups=mesh['ctx'=32,'tp'=8] {'ctx'}, dimensions={0}, use_global_device_ids=true | all-gather | bytes 540672 | tf_op jit(solution)/shard_map/all_gather | solution.py:75
  71.0 0.2 copy.24
  71.2 0.2 pad_add_fusion.1
  71.4 0.0 copy-start.3
  71.4 0.0 copy-start.4
  71.4 4.7 %fusion.7 = (f32[8,256]{1,0:T(8,128)S(1)}, f32[776,256,8]{1,0,2:T(8,128)}) fusion(pred[256,776]{0,1:T(8,128)(4,1)S(1)} %pad_add_fusion.1, bf16[256,8,128]{0,2,1:T(8,128)(2,1)S(1)} %bitcast.93, bf16[8,128]{1,0:T(8,128)(2,1)} %param.14, bf16[768,128]{1,0:T(8,128)(2,1)} %param.10), kind=kOutput, calls=%fused_computation.11 | convolution fusion | flops 412010496 | bytes 7286784 | tf_op jit(solution)/shard_map/qhgd,khd->hgqk/dot_general | solution.py:91
  76.1 59.3 %pmax.7 = f32[8,256]{1,0:T(8,128)S(1)} all-reduce(f32[8,256]{1,0:T(8,128)S(1)} %get-tuple-element.46), channel_id=1, replica_groups=mesh['ctx'=32,'tp'=8] {'ctx'}, use_global_device_ids=true, to_apply=%region_6.7 | all-reduce | flops 2048 | bytes 16384 | tf_op jit(solution)/shard_map/pmax | solution.py:117
  135.4 0.0 copy-start.1
  135.5 4.5 %fusion.8 = f32[8,256]{1,0:T(8,128)S(1)} fusion(f32[776,256,8]{1,0,2:T(8,128)} %get-tuple-element.47, f32[8,256]{1,0:T(8,128)S(1)} %get-tuple-element.46, pred[256,776]{0,1:T(8,128)(4,1)S(1)} %pad_add_fusion.1), kind=kLoop, calls=%fused_computation.13 | loop fusion | flops 7944192 | bytes 6572032 | tf_op jit(solution)/shard_map/reduce_sum | solution.py:23
  139.9 0.0 copy-done.3
  139.9 0.0 copy-done.4
  140.0 0.1 copy-done.1
  140.1 0.0 copy-start.2
  140.1 3.2 fusion.31
  143.3 0.0 all-reduce.7.cloned.1.call-update
  143.3 0.2 fusion.17
  143.5 0.7 fusion.42
  144.2 57.3 %psum.46 = f32[8,256]{1,0:T(8,128)S(1)} all-reduce(f32[8,256]{1,0:T(8,128)S(1)} %get-tuple-element.42), channel_id=1, replica_groups=mesh['ctx'=32,'tp'=8] {'ctx'}, use_global_device_ids=true, to_apply=%region_9.10 | all-reduce | flops 2048 | bytes 16384 | tf_op jit(solution)/shard_map/psum | solution.py:119
  201.6 1.6 pad_add_fusion
  203.1 0.0 all-reduce.9.cloned.1.call-done
  203.2 0.0 copy-done
  203.2 0.0 copy-done.2
  203.2 21.5 %fusion.56 = (f32[8,768]{1,0:T(8,128)}, bf16[8,768,1536]{1,2,0:T(8,128)(2,1)}) fusion(pred[768,1536]{0,1:T(8,128)(4,1)S(1)} %pad_add_fusion, bf16[768,128]{1,0:T(8,128)(2,1)S(1)} %copy-done.2, bf16[768,128]{1,0:T(8,128)(2,1)} %get-tuple-element.40, bf16[768,1024]{1,0:T(8,128)(2,1)S(1)} %copy-done), kind=kOutput, calls=%fused_computation.62 | convolution fusion | flops 2473330176 | bytes 22044672 | tf_op jit(solution)/shard_map/while/body/eval_jaxpr/sub | solution.py:22
  224.7 9.2 %fusion.16 = bf16[768,8,128]{0,2,1:T(8,128)(2,1)S(1)} fusion(bf16[8,768,1536]{1,2,0:T(8,128)(2,1)} %get-tuple-element.45, f32[768,8]{0,1:T(8,128)} %bitcast.96, bf16[768,128]{1,0:T(8,128)(2,1)} %param.11, bf16[768,128]{1,0:T(8,128)(2,1)} %get-tuple-element.41), kind=kOutput, calls=%fused_computation.20 | convolution fusion | flops 2418278400 | bytes 20865024 | tf_op jit(solution)/shard_map/while/body/eval_jaxpr/grk,kd->grd/dot_general | solution.py:49
  233.9 1.6 copy.26
  235.5 75.6 %all-reduce.7.cloned.1.call-done = f32[8,256,128]{2,1,0:T(8,128)} async-done(((f32[8,256,128]{2,1,0:T(8,128)}), f32[8,256,128]{2,1,0:T(8,128)}) %all-reduce.7.cloned.1.call-update) | async-done | bytes 1048592 | tf_op jit(solution)/shard_map/psum | solution.py:119
  311.2 1.8 convolution_bitcast_fusion
  313.0 28.7 %all-reduce.10 = bf16[256,256]{1,0:T(8,128)(2,1)} all-reduce(f32[256,256]{1,0:T(8,128)S(1)} %convolution_bitcast_fusion), channel_id=1, replica_groups=mesh['ctx'=32,'tp'=8] {'tp'}, use_global_device_ids=true, to_apply=%region_10.11 | all-reduce | flops 65536 | bytes 393216 | tf_op jit(solution)/shard_map/psum | solution.py:125
  (5 shorter events, 0.0 us)
Async XLA Ops:
  7.2 196.0 %copy-start = (bf16[768,1024]{1,0:T(8,128)(2,1)S(1)}, bf16[768,1024]{1,0:T(8,128)(2,1)}, u32[]{:S(2)}) copy-start(bf16[768,1024]{1,0:T(8,128)(2,1)} %param.9) | copy-start | bytes 4718596
  7.2 196.0 %all-reduce.9.cloned.1.call-start = ((), (), s32[]{:S(2)}) async-start(), calls=%async_computation.1 | async-start | bytes 786432 | tf_op jit(solution)/shard_map/psum | solution.py:16
  10.6 300.6 %all-reduce.7.cloned.1.call-start = ((), (), s32[]{:S(2)}) async-start(), calls=%async_computation | async-start | bytes 2097152 | tf_op jit(solution)/shard_map/psum | solution.py:119
  71.4 68.5 %copy-start.3 = (bf16[768,128]{1,0:T(8,128)(2,1)S(1)}, bf16[768,128]{1,0:T(8,128)(2,1)}, u32[]{:S(2)}) copy-start(bf16[768,128]{1,0:T(8,128)(2,1)} %param.11) | copy-start | bytes 589828
  71.4 68.5 %copy-start.4 = (bf16[8,128]{1,0:T(8,128)(2,1)S(1)}, bf16[8,128]{1,0:T(8,128)(2,1)}, u32[]{:S(2)}) copy-start(bf16[8,128]{1,0:T(8,128)(2,1)} %param.15) | copy-start | bytes 6148
  135.4 4.7 %copy-start.1 = (f32[776,256,8]{1,0,2:T(8,128)S(1)}, f32[776,256,8]{1,0,2:T(8,128)}, u32[]{:S(2)}) copy-start(f32[776,256,8]{1,0,2:T(8,128)} %get-tuple-element.47) | copy-start | bytes 19070980
  140.1 63.1 %copy-start.2 = (bf16[768,128]{1,0:T(8,128)(2,1)S(1)}, bf16[768,128]{1,0:T(8,128)(2,1)}, u32[]{:S(2)}) copy-start(bf16[768,128]{1,0:T(8,128)(2,1)} %param.10) | copy-start | bytes 589828
Sparse Core Ops, SparseCore 0:
  12.0 144.7 all-reduce.8
  160.7 150.4 all-reduce.6
where the time goes:
time: 349 us
  blocking collectives  201 us (58%)
  waiting for transfers between devices  75.7 us (22%)
  matrix products  40.4 us (12%)
  between operations  15.6 us (4%)
  other arithmetic  11.2 us (3%)
  local copies, waits for them, and re-layouts  4.22 us (1%)
    psum x1, waiting for transfers between devices, body(): lax.psum((total * factor, summed * factor[..., None]), 'ctx')  75.6 us
    pmax x1, blocking collectives, body(): merged_max = lax.pmax(highest, 'ctx')  59.3 us
    psum x1, blocking collectives, body(): lax.psum((total * factor, summed * factor[..., None]), 'ctx')  57.3 us
    all_gather x1, blocking collectives, body(): lax.all_gather(question_queries, 'ctx', axis=0, tiled=True)  36.4 us
    psum x1, blocking collectives, body(): answer = lax.psum(partial_answer, 'tp').astype(jnp.bfloat16)  28.7 us
    sub x1, matrix products, softmax_parts(): weights = jnp.where(visible, jnp.exp(masked - highest[..., None]), 0.0)  21.5 us
    psum x1, blocking collectives, broadcast(): return lax.psum(block, axis)  19.6 us
    dot_general x1, matrix products, encode_head(): jnp.einsum('grk,kd->grd', rounded, values_all, preferred_element_type=jnp...  9.19 us
  transfers between devices with their start and end apart: 2, of which 1 were waited for; matrix products, arithmetic and copies ran while one was open for 14% of the time, Pallas kernels for 0%

commit v1 on v0

v1 whole, which is shorter than its diff:
```python
import functools
import math

import jax
import jax.numpy as jnp
from jax import lax
from jax.experimental import pallas as pl
from jax.experimental.pallas import tpu as pltpu
from jax.sharding import PartitionSpec as P

MESH = pl.DeviceIdType.MESH
NT = (((1,), (1,)), ((), ()))
BF = jnp.bfloat16
F32 = jnp.float32
NEG = -1e30
HD = 128
HEADS = 8
NY, NZ, TP = 4, 8, 8
ROWS = 768
QROWS = 8
TILE = 256
NRB = ROWS // TILE
SL = ROWS * 2 // (NY * NZ)
QUARTER = SL * NZ
SCALE = math.log2(math.e) / math.sqrt(HD)
LOG2E = math.log2(math.e)
ZORDER = (1, 7, 2, 6, 3, 5, 4)
YORDER = (1, 3, 2)
HG = 4

S_Q, S_SM, S_KV, S_AA, S_AB, S_AC, S_AD = 0, 7, 10, 16, 23, 26, 33
S_PZ, S_TZ, S_TY, S_RX, S_GX = 36, 43, 50, 74, 81
N_SEM = 88


def live_keys(live, keys, kk, values, va, rows):
    kk[rows, :] = keys
    va[rows, :HD] = jnp.where(live, values, jnp.zeros_like(values))
    va[rows, HD:] = jnp.where(live, 1.0, 0.0).astype(BF)


def kernel(
    cq, ck, cv, blen, qq, qk, qv, qpos, w,
    out, ans,
    cqv, wv, kvb, kk, va, akk, ava, bias,
    mo, acco, obuf,
    qbuf, sml, rst, ast, akv,
    p2kk, p2va, m2, acc2,
    cmsg, crecv, abuf, pown, psend, prec, ansb,
    ss, rs, ls,
):
    ctx = lax.axis_index("ctx")
    t = lax.axis_index("tp")
    y, z = ctx // NZ, lax.rem(ctx, NZ)

    def at_z(d):
        return lax.rem(z + d + NZ, NZ)

    def at_y(d):
        return lax.rem(y + d + NY, NY)

    def at_t(d):
        return lax.rem(t + d + TP, TP)

    def dev(yy, zz, tt):
        return (yy * NZ + zz, tt)

    def remote(src, dst, si, ri, device):
        return pltpu.make_async_remote_copy(
            src_ref=src, dst_ref=dst, send_sem=ss.at[si], recv_sem=rs.at[ri],
            device_id=device, device_id_type=MESH,
        )

    def recv(dst, ri):
        remote(dst, dst, ri, ri, dev(at_y(1), z, t)).wait_recv()

    sends = []

    def send(src, dst, si, device):
        copy = remote(src, dst, si, si, device)
        copy.start()
        sends.append(copy)

    barrier = pltpu.get_barrier_semaphore()
    peers = (
        [dev(y, at_z(d), t) for d in range(1, NZ)]
        + [dev(at_y(d), z, t) for d in range(1, NY)]
        + [dev(y, z, at_t(d)) for d in range(1, TP)]
    )
    for peer in peers:
        pl.semaphore_signal(barrier, inc=1, device_id=peer, device_id_type=MESH)
    loads = [
        pltpu.make_async_copy(src.at[pl.ds(i * QUARTER, QUARTER)], kvb.at[y, 2 * n + i], ls.at[2 * n + i])
        for n, src in enumerate((ck, cv)) for i in range(2)
    ]
    for copy in loads:
        copy.start()
    load_q = pltpu.make_async_copy(cq, cqv, ls.at[4])
    load_q.start()
    load_w = pltpu.make_async_copy(w, wv, ls.at[5])
    load_w.start()

    row8 = lax.broadcasted_iota(jnp.int32, (8, HD), 0)
    lane8 = lax.broadcasted_iota(jnp.int32, (8, HD), 1)
    qf = qq[...].astype(F32)
    qbuf[z, 0:64, :] = jnp.concatenate([qf[:, h * HD:(h + 1) * HD] for h in range(HEADS)], axis=0).astype(BF)
    pos = jnp.zeros((8, HD), jnp.int32)
    key_pos = jnp.full((8, HD), 512, jnp.int32)
    for r in range(QROWS):
        pos = jnp.where(row8 == r, qpos[r], pos)
        key_pos = jnp.where(lane8 == y * QROWS + r, qpos[r], key_pos)
    pos = pos.astype(F32)
    key_pos = key_pos.astype(F32)
    qbuf[z, 64:80, :] = jnp.concatenate([pos, pos], axis=0).astype(BF)
    length = jnp.zeros((8, HD), jnp.int32) + blen[0]
    info = jnp.concatenate([length // 128, lax.rem(length, 128)], axis=0).astype(F32).astype(BF)
    sml[y, 0:16, :] = jnp.concatenate([qk[...].astype(F32), qv[...].astype(F32)], axis=0).astype(BF)
    sml[y, 16:32, :] = jnp.concatenate([key_pos, key_pos], axis=0).astype(BF)
    sml[y, 32:48, :] = info

    for copy in loads:
        copy.wait()
    pl.semaphore_wait(barrier, len(peers))

    for d in ZORDER:
        send(qbuf.at[z], qbuf.at[z], S_Q + d - 1, dev(y, at_z(d), t))
    up, down = dev(at_y(1), z, t), dev(at_y(3), z, t)
    keys, values = pl.ds(0, 2), pl.ds(2, 2)
    send(kvb.at[y, keys], kvb.at[y, keys], S_KV, up)
    send(kvb.at[y, values], kvb.at[y, values], S_KV + 2, down)
    for d in YORDER:
        send(sml.at[y], sml.at[y], S_SM + d - 1, dev(at_y(d), z, t))
    send(kvb.at[y, values], kvb.at[y, values], S_KV + 1, up)
    send(kvb.at[y, keys], kvb.at[y, keys], S_KV + 3, down)

    root = (y == 0) & (z == 0)

    @pl.when(root)
    def _():
        for j in range(NZ):
            for i in range(4):
                rst[j, i, 0:SL, :] = kvb[0, i, j * SL:(j + 1) * SL, :]
                rst[j, i, SL:SL + 16, :] = info
        ast[...] = rst[0]
        for j in range(1, NZ):
            remote(rst.at[j], ast, S_AA + j - 1, S_AA, dev(0, j, t)).start()

    row_of = lax.broadcasted_iota(jnp.int32, (QUARTER, HD), 0)
    for i in range(2):
        live = row_of + i * QUARTER < blen[0]
        live_keys(
            live, jnp.where(live, kvb[y, i], kvb[y, 0, 0:1, :]), kk, kvb[y, 2 + i], va,
            slice(i * QUARTER, (i + 1) * QUARTER),
        )
    rr = lax.broadcasted_iota(jnp.int32, (TILE, TILE), 0)
    cc = lax.broadcasted_iota(jnp.int32, (TILE, TILE), 1)
    bias[...] = jnp.where(cc <= rr, 0.0, NEG)
    load_q.wait()

    def own_step(rb, h):
        qt = cqv[rb * TILE:(rb + 1) * TILE, pl.ds(pl.multiple_of(h * HD, HD), HD)]
        diagonal = slice(rb * TILE, (rb + 1) * TILE)
        sd = lax.dot_general(qt, kk[diagonal], NT, preferred_element_type=F32) + bias[...]
        top = jnp.max(sd, axis=1, keepdims=True)
        if rb:
            so = lax.dot_general(qt, kk[0:rb * TILE], NT, preferred_element_type=F32)
            top = jnp.maximum(top, jnp.max(so, axis=1, keepdims=True))
        top_s = top * SCALE
        pd = jnp.exp2(sd * SCALE - top_s).astype(BF)
        acc = jnp.dot(pd, va[diagonal], preferred_element_type=F32)
        if rb:
            po = jnp.exp2(so * SCALE - top_s).astype(BF)
            acc = acc + jnp.dot(po, va[0:rb * TILE], preferred_element_type=F32)
        acco[rb * HEADS + h] = acc
        mo[rb * HEADS + h] = jnp.broadcast_to(top_s, (TILE, HD))

    def own_steps(rb):
        @pl.loop(0, HEADS // HG)
        def _(i):
            for u in range(HG):
                own_step(rb, i * HG + u)

    own_steps(0)
    own_steps(1)


    @pl.when(y == 0)
    def _():
        @pl.when(z != 0)
        def _():
            recv(ast, S_AA)
        akv[0, z] = ast[0]
        for d in range(1, NY):
            remote(ast.at[d], akv.at[d, z], S_AB + d - 1, S_AB, dev(d, z, t)).start()

    own_steps(2)

    below, above, opposite = at_y(3), at_y(1), at_y(2)
    recv(kvb.at[below, keys], S_KV)
    send(kvb.at[below, keys], kvb.at[below, keys], S_KV + 4, up)
    recv(kvb.at[above, values], S_KV + 2)
    send(kvb.at[above, values], kvb.at[above, values], S_KV + 5, down)

    @pl.when(y != 0)
    def _():
        recv(akv.at[y, z], S_AB)

    for d in ZORDER:
        send(akv.at[y, z], akv.at[y, z], S_AC + d - 1, dev(y, at_z(d), t))

    for d in range(1, NZ):
        recv(qbuf.at[at_z(-d)], S_Q + d - 1)
    for d in range(1, NY):
        recv(sml.at[at_y(-d)], S_SM + d - 1)
    half = NZ // 2 * 64

    def asked(i):
        return jnp.concatenate([qbuf[i * 4 + j, 0:64, :] for j in range(4)], axis=0)

    small = [sml[j].astype(F32) for j in range(NY)]
    zero96 = jnp.zeros((HD - NY * QROWS, HD), F32)
    ext_k = jnp.concatenate([s[0:8] for s in small] + [zero96], axis=0).astype(BF)
    ext_v = jnp.concatenate([s[8:16] for s in small] + [zero96], axis=0).astype(BF)
    ext_va = jnp.concatenate([ext_v, jnp.ones((HD, HD), BF)], axis=1)
    ext_pos = functools.reduce(jnp.minimum, [s[16:17] for s in small])

    for i in range(2):
        qt = asked(i)
        rows_pos = jnp.concatenate(
            [p for j in range(4) for p in [qbuf[i * 4 + j, 64:80, :].astype(F32)[0:8]] * HEADS], axis=0
        )
        se = lax.dot_general(qt, ext_k, NT, preferred_element_type=F32)
        se = jnp.where(ext_pos <= rows_pos, se, NEG)
        sa = lax.dot_general(qt, kk[...], NT, preferred_element_type=F32)
        top = jnp.maximum(jnp.max(se, axis=1, keepdims=True), jnp.max(sa, axis=1, keepdims=True)) * SCALE
        acc = jnp.dot(jnp.exp2(sa * SCALE - top).astype(BF), va[...], preferred_element_type=F32)
        acc = acc + jnp.dot(jnp.exp2(se * SCALE - top).astype(BF), ext_va, preferred_element_type=F32)
        m2[i * half:(i + 1) * half] = jnp.broadcast_to(top, (half, HD))
        acc2[i * half:(i + 1) * half] = acc

    def phase_two(slot):
        length = (sml[slot, 32:48, :].astype(F32))
        live_to = length[0:1] * 128.0 + length[8:9]
        for i in range(2):
            live = (row_of + i * QUARTER).astype(F32) < live_to
            live_keys(
                live, jnp.where(live, kvb[slot, i], kvb[slot, 0, 0:1, :]), p2kk, kvb[slot, 2 + i], p2va,
                slice(i * QUARTER, (i + 1) * QUARTER),
            )
        for i in range(2):
            part = slice(i * half, (i + 1) * half)
            sa = lax.dot_general(asked(i), p2kk[...], NT, preferred_element_type=F32)
            old = m2[part]
            top = jnp.maximum(jnp.max(sa, axis=1, keepdims=True) * SCALE, old)
            acc = jnp.dot(jnp.exp2(sa * SCALE - top[:, 0:1]).astype(BF), p2va[...], preferred_element_type=F32)
            keep = jnp.exp2(old - top)
            acc2[part] = acc + acc2[part] * jnp.concatenate([keep, keep], axis=1)
            m2[part] = top

    recv(kvb.at[below, values], S_KV + 1)
    phase_two(below)
    recv(kvb.at[above, keys], S_KV + 3)
    phase_two(above)

    for d in range(1, NZ):
        recv(akv.at[y, at_z(-d)], S_AC + d - 1)
    data = pl.ds(0, SL)
    for d in YORDER:
        send(akv.at[y, :, data], akv.at[y, :, data], S_AD + d - 1, dev(at_y(d), z, t))

    recv(kvb.at[opposite, keys], S_KV + 4)
    recv(kvb.at[opposite, values], S_KV + 5)
    phase_two(opposite)

    total = acc2[:, HD:]
    lse = m2[...] + jnp.log(total) * LOG2E
    part_out = acc2[:, :HD] / total
    for j in range(NZ):
        compact = jnp.zeros((8, HD), F32)
        for h in range(HEADS):
            compact = jnp.where(lane8 == h, lse[j * 64 + h * 8:j * 64 + h * 8 + 8], compact)
        first = compact.astype(BF).astype(F32)
        second = (compact - first).astype(BF).astype(F32)
        third = compact - first - second
        cmsg[j, 0:64, :] = part_out[j * 64:(j + 1) * 64].astype(BF)
        cmsg[j, 64:96, :] = jnp.concatenate([first, second, third, jnp.zeros((8, HD), F32)], axis=0).astype(BF)
    for d in ZORDER:
        send(cmsg.at[at_z(d)], crecv.at[z], S_PZ + d - 1, dev(y, at_z(d), t))

    for d in range(1, NY):
        recv(akv.at[at_y(-d), :, data], S_AD + d - 1)
    alen = akv[y, z, SL:SL + 16, :].astype(F32)
    alive_to = jnp.where(ctx == 0, 0.0, alen[0:1] * 128.0 + alen[8:9])
    for i in range(2):
        live = (row_of + i * QUARTER).astype(F32) < alive_to
        live_keys(
            live,
            jnp.where(live, akv[i, :, 0:SL, :].reshape(QUARTER, HD), akv[0, 0, 0:1, :]),
            akk,
            akv[2 + i, :, 0:SL, :].reshape(QUARTER, HD),
            ava,
            slice(i * QUARTER, (i + 1) * QUARTER),
        )

    def anchor_step(rb, h):
        cols = pl.ds(pl.multiple_of(h * HD, HD), HD)
        rows = slice(rb * TILE, (rb + 1) * TILE)
        sa = lax.dot_general(cqv[rows, cols], akk[...], NT, preferred_element_type=F32)
        old = mo[rb * HEADS + h]
        top = jnp.maximum(jnp.max(sa, axis=1, keepdims=True) * SCALE, old)
        acc = jnp.dot(jnp.exp2(sa * SCALE - top[:, 0:1]).astype(BF), ava[...], preferred_element_type=F32)
        keep = jnp.exp2(old - top)
        acc = acc + acco[rb * HEADS + h] * jnp.concatenate([keep, keep], axis=1)
        obuf[rows, cols] = (acc[:, :HD] / acc[:, HD:]).astype(BF)

    stores = [
        pltpu.make_async_copy(
            obuf.at[pl.ds(rb * TILE, TILE)], out.at[pl.ds(rb * TILE, TILE)], ls.at[6 + rb]
        )
        for rb in range(NRB)
    ]

    def anchor_steps(rb):
        @pl.loop(0, HEADS // HG)
        def _(i):
            for u in range(HG):
                anchor_step(rb, i * HG + u)

        stores[rb].start()

    anchor_steps(0)
    anchor_steps(1)

    for d in range(1, NZ):
        recv(crecv.at[at_z(-d)], S_PZ + d - 1)
    parts = [cmsg[z].astype(F32)] + [crecv[at_z(-d)].astype(F32) for d in range(1, NZ)]
    lses = [p[64:72] + p[72:80] + p[80:88] for p in parts]
    top = functools.reduce(jnp.maximum, lses)
    weights = [jnp.exp2(x - top) for x in lses]
    weight_sum = functools.reduce(jnp.add, weights)
    weights = [x / weight_sum for x in weights]
    merged = []
    for h in range(HEADS):
        merged.append(functools.reduce(
            jnp.add, [x[:, h:h + 1] * p[h * 8:h * 8 + 8] for x, p in zip(weights, parts)]
        ))
    merged = jnp.concatenate(
        [jnp.concatenate(merged[0:4], axis=1), jnp.concatenate(merged[4:8], axis=1)], axis=0
    )
    abuf[y, z] = merged.astype(BF)

    for d in ZORDER:
        send(abuf.at[y, z], abuf.at[y, z], S_TZ + d - 1, dev(y, at_z(d), t))
    for k in (0,) + ZORDER:
        zz = at_z(-k)
        if k:
            recv(abuf.at[y, zz], S_TZ + k - 1)
        for d in YORDER:
            send(abuf.at[y, zz], abuf.at[y, zz], S_TY + 3 * k + d - 1, dev(at_y(d), z, t))

    anchor_steps(2)
    load_w.wait()
    for k in range(NZ):
        for d in range(1, NY):
            recv(abuf.at[at_y(-d), at_z(-k)], S_TY + 3 * k + d - 1)

    rows = abuf[...].reshape(NY * NZ * 16, 4 * HD)
    low = jnp.dot(rows, wv[0:4 * HD], preferred_element_type=F32).reshape(NY * NZ, 16, -1)
    high = jnp.dot(rows, wv[4 * HD:], preferred_element_type=F32).reshape(NY * NZ, 16, -1)
    partial = (low[:, 0:8] + high[:, 8:16]).reshape(pown.shape)
    pown[...] = partial
    psend[...] = partial.astype(BF)
    for d in range(1, TP):
        send(psend.at[at_t(d)], prec.at[t], S_RX + d - 1, dev(y, z, at_t(d)))
    for d in range(1, TP):
        recv(prec.at[at_t(-d)], S_RX + d - 1)
    answer = pown[t]
    for d in range(1, TP):
        answer = answer + prec[at_t(-d)].astype(F32)
    ansb[t] = answer.astype(BF)
    for d in range(1, TP):
        send(ansb.at[t], ansb.at[t], S_GX + d - 1, dev(y, z, at_t(d)))
    for d in range(1, TP):
        recv(ansb.at[at_t(-d)], S_GX + d - 1)
    ans[...] = ansb[...].reshape(ans.shape)

    for copy in sends:
        copy.wait_send()

    @pl.when(root)
    def _():
        for j in range(1, NZ):
            remote(rst.at[j], ast, S_AA + j - 1, S_AA, dev(0, j, t)).wait_send()

    @pl.when(y == 0)
    def _():
        for d in range(1, NY):
            remote(ast.at[d], akv.at[d, z], S_AB + d - 1, S_AB, dev(d, z, t)).wait_send()

    for copy in stores:
        copy.wait()


def body(cq, ck, cv, blen, qq, qk, qv, qpos, w):
    hbm = pl.BlockSpec(memory_space=pl.ANY)
    vmem = pl.BlockSpec(memory_space=pltpu.VMEM)
    smem = pl.BlockSpec(memory_space=pltpu.SMEM)
    columns = w.shape[1]
    v = pltpu.VMEM
    return pl.pallas_call(
        kernel,
        out_shape=(
            jax.ShapeDtypeStruct(cq.shape, BF),
            jax.ShapeDtypeStruct((NY * NZ * QROWS, columns), BF),
        ),
        in_specs=[hbm, hbm, hbm, smem, vmem, vmem, vmem, smem, hbm],
        out_specs=(hbm, vmem),
        scratch_shapes=[
            v(cq.shape, BF),
            v(w.shape, BF),
            v((NY, 4, QUARTER, HD), BF),
            v((ROWS, HD), BF),
            v((ROWS, 2 * HD), BF),
            v((ROWS, HD), BF),
            v((ROWS, 2 * HD), BF),
            v((TILE, TILE), F32),
            v((NRB * HEADS, TILE, HD), F32),
            v((NRB * HEADS, TILE, 2 * HD), F32),
            v(cq.shape, BF),
            v((NZ, 80, HD), BF),
            v((NY, 48, HD), BF),
            v((NZ, 4, SL + 16, HD), BF),
            v((4, SL + 16, HD), BF),
            v((4, NZ, SL + 16, HD), BF),
            v((ROWS, HD), BF),
            v((ROWS, 2 * HD), BF),
            v((NZ * 64, HD), F32),
            v((NZ * 64, 2 * HD), F32),
            v((NZ, 96, HD), BF),
            v((NZ, 96, HD), BF),
            v((NY, NZ, 16, 4 * HD), BF),
            v((TP, NY * NZ, columns), F32),
            v((TP, NY * NZ, columns), BF),
            v((TP, NY * NZ, columns), BF),
            v((TP, NY * NZ, columns), BF),
            pltpu.SemaphoreType.DMA((N_SEM,)),
            pltpu.SemaphoreType.DMA((N_SEM,)),
            pltpu.SemaphoreType.DMA((9,)),
        ],
        compiler_params=pltpu.CompilerParams(
            collective_id=1, has_side_effects=True, vmem_limit_bytes=48 * 2**20
        ),
        name="star_attention",
    )(cq, ck, cv, blen, qq, qk, qv, qpos, w)


def solution(mesh):
    in_specs = (
        P("ctx", "tp"),
        P("ctx", "tp"),
        P("ctx", "tp"),
        P("ctx"),
        P("ctx", "tp"),
        P("ctx", "tp"),
        P("ctx", "tp"),
        P("ctx"),
        P("tp", "ctx"),
    )
    out_specs = (P("ctx", "tp"), P(None, "ctx"))
    return jax.shard_map(body, mesh=mesh, in_specs=in_specs, out_specs=out_specs, check_vma=False)
```

time: 349 us -> 71.7 us (0.21)
  blocking collectives: 201 us -> 0 us
  waiting for transfers between devices: 75.7 us -> 0 us
  Pallas kernels: 0 us -> 61.2 us
  matrix products: 40.4 us -> 0 us
  between operations: 15.6 us -> 1.3 us
  other arithmetic: 11.2 us -> 0 us
  local copies, waits for them, and re-layouts: 4.22 us -> 8.83 us
    psum x3 -> x0, blocking collectives: 106 us -> none  [the longest x1 57.3 us: body(): lax.psum((total * factor, summed * factor[..., None]), 'ctx')]
    psum x2 -> x0, waiting for transfers between devices: 75.7 us -> none  [the longest x1 75.6 us: body(): lax.psum((total * factor, summed * factor[..., None]), 'ctx')]
    pallas_call x0 -> x1, Pallas kernels: none -> 61.2 us  [body(): pl.pallas_call(kernel, out_shape=(jax.ShapeDtypeStruct(cq.shape, BF), jax...]
    pmax x1 -> x0, blocking collectives: 59.3 us -> none  [body(): merged_max = lax.pmax(highest, 'ctx')]
    all_gather x1 -> x0, blocking collectives: 36.4 us -> none  [body(): lax.all_gather(question_queries, 'ctx', axis=0, tiled=True)]
    sub x1 -> x0, matrix products: 21.5 us -> none  [softmax_parts(): weights = jnp.where(visible, jnp.exp(masked - highest[..., None]), 0.0)]
    dot_general x4 -> x0, matrix products: 18.9 us -> none  [the longest x1 9.19 us: encode_head(): jnp.einsum('grk,kd->grd', rounded, values_all, preferred_element_type=jnp...]
    unnamed x14 -> x18, local copies, waits for them, and re-layouts: 4 us -> 8.83 us
  transfers between devices with their start and end apart: 2 -> 0, of which waited for: 1 -> 0; matrix products, arithmetic and copies ran while one was open for 14% -> 0% of each run, Pallas kernels for 0% -> 0%
where the time goes in v1:
time: 71.7 us; the launch traced here: 71.4 us
  Pallas kernels  61.2 us (85%)
  local copies, waits for them, and re-layouts  8.83 us (12%)
  between operations  1.3 us (2%)
    pallas_call x1, Pallas kernels, body(): pl.pallas_call(kernel, out_shape=(jax.ShapeDtypeStruct(cq.shape, BF), jax...  61.2 us
    unnamed x18, local copies, waits for them, and re-layouts  8.83 us

profile of v1, /device:TPU:1, one launch (start us, length us, event | category | flops | bytes accessed | tf_op | source)
XLA Modules:
  0.0 71.4 jit_solution(1558269527837488400)
XLA Ops:
  1.3 0.0 copy-start
  1.3 1.4 %copy-done = bf16[768,1024]{1,0:T(8,128)(2,1)S(1)} copy-done((bf16[768,1024]{1,0:T(8,128)(2,1)S(1)}, bf16[768,1024]{1,0:T(8,128)(2,1)}, u32[]{:S(2)}) %copy-start) | copy-done | bytes 1572888
  2.7 0.0 copy-start.1
  2.7 1.0 %copy-done.1 = bf16[1024,256]{1,0:T(8,128)(2,1)S(1)} copy-done((bf16[1024,256]{1,0:T(8,128)(2,1)S(1)}, bf16[1024,256]{1,0:T(8,128)(2,1)}, u32[]{:S(2)}) %copy-start.1) | copy-done | bytes 524312
  3.7 0.0 copy-start.2
  3.7 0.9 %copy-done.2 = bf16[768,128]{1,0:T(8,128)(2,1)S(1)} copy-done((bf16[768,128]{1,0:T(8,128)(2,1)S(1)}, bf16[768,128]{1,0:T(8,128)(2,1)}, u32[]{:S(2)}) %copy-start.2) | copy-done | bytes 196632
  4.7 0.0 copy-start.3
  4.7 0.9 %copy-done.3 = bf16[768,128]{1,0:T(8,128)(2,1)S(1)} copy-done((bf16[768,128]{1,0:T(8,128)(2,1)S(1)}, bf16[768,128]{1,0:T(8,128)(2,1)}, u32[]{:S(2)}) %copy-start.3) | copy-done | bytes 196632
  5.6 0.0 copy-start.4
  5.6 0.7 %copy-done.4 = bf16[8,1024]{1,0:T(8,128)(2,1)S(1)} copy-done((bf16[8,1024]{1,0:T(8,128)(2,1)S(1)}, bf16[8,1024]{1,0:T(8,128)(2,1)}, u32[]{:S(2)}) %copy-start.4) | copy-done | bytes 16408
  6.3 0.0 copy-start.5
  6.3 0.7 copy-done.5
  7.0 0.0 copy-start.6
  7.0 0.7 copy-done.6
  7.7 0.0 copy-start.7
  7.7 0.7 copy-done.7
  8.3 61.2 %star_attention.1 = (bf16[768,1024]{1,0:T(8,128)(2,1)S(1)}, bf16[256,256]{1,0:T(8,128)(2,1)S(1)}) custom-call(bf16[768,1024]{1,0:T(8,128)(2,1)S(1)} %copy-done, bf16[768,128]{1,0:T(8,128)(2,1)S(1)} %copy-done.2, bf16[768,128]{1,0:T(8,128)(2,1)S(1)} %copy-done.3, s32[1]{0:T(128)S(6)} %copy.13.blen, bf16[8,1024]{1,0:T(8,128)(2,1)S(1)} %copy-done.4, ...), custom_call_target="tpu_custom_call" | custom-call | tf_op jit(solution)/shard_map/star_attention/pallas_call | solution.py:410
  69.5 1.1 %copy.14 = bf16[768,1024]{1,0:T(8,128)(2,1)} copy(bf16[768,1024]{1,0:T(8,128)(2,1)S(1)} %get-tuple-element.4) | data formatting | bytes 3145728
  70.7 0.7 copy.15
Async XLA Ops:
  1.3 1.4 %copy-start = (bf16[768,1024]{1,0:T(8,128)(2,1)S(1)}, bf16[768,1024]{1,0:T(8,128)(2,1)}, u32[]{:S(2)}) copy-start(bf16[768,1024]{1,0:T(8,128)(2,1)} %cq.1) | copy-start | bytes 4718596
  2.7 1.0 %copy-start.1 = (bf16[1024,256]{1,0:T(8,128)(2,1)S(1)}, bf16[1024,256]{1,0:T(8,128)(2,1)}, u32[]{:S(2)}) copy-start(bf16[1024,256]{1,0:T(8,128)(2,1)} %w.1) | copy-start | bytes 1572868
  3.7 0.9 %copy-start.2 = (bf16[768,128]{1,0:T(8,128)(2,1)S(1)}, bf16[768,128]{1,0:T(8,128)(2,1)}, u32[]{:S(2)}) copy-start(bf16[768,128]{1,0:T(8,128)(2,1)} %ck.1) | copy-start | bytes 589828
  4.7 0.9 %copy-start.3 = (bf16[768,128]{1,0:T(8,128)(2,1)S(1)}, bf16[768,128]{1,0:T(8,128)(2,1)}, u32[]{:S(2)}) copy-start(bf16[768,128]{1,0:T(8,128)(2,1)} %cv.1) | copy-start | bytes 589828
  5.6 0.7 %copy-start.4 = (bf16[8,1024]{1,0:T(8,128)(2,1)S(1)}, bf16[8,1024]{1,0:T(8,128)(2,1)}, u32[]{:S(2)}) copy-start(bf16[8,1024]{1,0:T(8,128)(2,1)} %qq.1) | copy-start | bytes 49156
  6.3 0.7 copy-start.5
  7.0 0.7 copy-start.6
  7.7 0.7 copy-start.7

commit v2 on v1

v2 whole, which is shorter than its diff:
```python
import functools
import math

import jax
import jax.numpy as jnp
from jax import lax
from jax.experimental import pallas as pl
from jax.experimental.pallas import tpu as pltpu
from jax.sharding import PartitionSpec as P

MESH = pl.DeviceIdType.MESH
NT = (((1,), (1,)), ((), ()))
BF = jnp.bfloat16
F32 = jnp.float32
NEG = -1e30
HD = 128
HEADS = 8
NY, NZ, TP = 4, 8, 8
ROWS = 768
QROWS = 8
TILE = 256
NRB = ROWS // TILE
SL = ROWS * 2 // (NY * NZ)
THIRD = ROWS // 3
SCALE = math.log2(math.e) / math.sqrt(HD)
LOG2E = math.log2(math.e)
ZORDER = (1, 7, 2, 6, 3, 5, 4)
YORDER = (1, 3, 2)
HG = 4

S_Q, S_SM, S_KV, S_AA, S_AB, S_AC, S_AD = 0, 7, 10, 16, 23, 26, 33
S_PZ, S_TZ, S_TY, S_RX, S_GX = 36, 43, 50, 74, 81
N_SEM = 88


def kernel(
    cq, ck, cv, blen, qq_hbm, qk_hbm, qv_hbm, qpos, w,
    out, ans,
    qq, qk, qv, cqv, wv, kvb, kk, va, akk, ava, bias,
    mo, acco, obuf,
    qbuf, sml, rst, ast, akv,
    p2kk, p2va, m2, acc2,
    cmsg, crecv, abuf, pown, psend, prec, ansb,
    ss, rs, ls,
):
    ctx = lax.axis_index("ctx")
    t = lax.axis_index("tp")
    z = lax.rem(ctx, NZ)
    c = lax.rem(ctx // NZ + 2 * z, NY)

    def at_z(d):
        return lax.rem(z + d + NZ, NZ)

    def at_c(d):
        return lax.rem(c + d + NY, NY)

    def at_t(d):
        return lax.rem(t + d + TP, TP)

    def dev(cc, zz, tt):
        return (lax.rem(cc + 2 * zz, NY) * NZ + zz, tt)

    def z_to(d):
        return at_z(-1) if d == 2 else z

    def z_from(d):
        return at_z(1) if d == 2 else z

    def next_to(d):
        return dev(at_c(d), z_to(d), t)

    def remote(src, dst, si, ri, device):
        return pltpu.make_async_remote_copy(
            src_ref=src, dst_ref=dst, send_sem=ss.at[si], recv_sem=rs.at[ri],
            device_id=device, device_id_type=MESH,
        )

    def recv(dst, ri):
        remote(dst, dst, ri, ri, next_to(1)).wait_recv()

    sends = []

    def send(src, dst, si, device):
        copy = remote(src, dst, si, si, device)
        copy.start()
        sends.append(copy)

    barrier = pltpu.get_barrier_semaphore()
    peers = (
        [dev(c, at_z(d), t) for d in range(1, NZ)]
        + [dev(at_c(1), z, t), dev(at_c(3), z, t), dev(at_c(2), at_z(1), t), dev(at_c(2), at_z(-1), t)]
        + [dev(c, z, at_t(d)) for d in range(1, TP)]
    )
    for peer in peers:
        pl.semaphore_signal(barrier, inc=1, device_id=peer, device_id_type=MESH)
    small_loads = [
        pltpu.make_async_copy(src, dst, ls.at[n])
        for n, (src, dst) in enumerate(((qq_hbm, qq), (qk_hbm, qk), (qv_hbm, qv)))
    ]
    loads = [
        pltpu.make_async_copy(src.at[pl.ds(a * THIRD, THIRD)], kvb.at[c, a, n], ls.at[3 + 2 * a + n])
        for a in range(3) for n, src in enumerate((ck, cv))
    ]
    load_q = pltpu.make_async_copy(cq, cqv, ls.at[9])
    load_w = pltpu.make_async_copy(w, wv, ls.at[10])
    for copy in small_loads + loads + [load_q, load_w]:
        copy.start()
    for copy in small_loads:
        copy.wait()

    row8 = lax.broadcasted_iota(jnp.int32, (8, HD), 0)
    lane8 = lax.broadcasted_iota(jnp.int32, (8, HD), 1)
    qf = qq[...].astype(F32)
    qbuf[z, 0:64, :] = jnp.concatenate([qf[:, h * HD:(h + 1) * HD] for h in range(HEADS)], axis=0).astype(BF)
    pos = jnp.zeros((8, HD), jnp.int32)
    key_pos = jnp.full((8, HD), 512, jnp.int32)
    for r in range(QROWS):
        pos = jnp.where(row8 == r, qpos[r], pos)
        key_pos = jnp.where(lane8 == c * QROWS + r, qpos[r], key_pos)
    pos = pos.astype(F32)
    key_pos = key_pos.astype(F32)
    qbuf[z, 64:80, :] = jnp.concatenate([pos, pos], axis=0).astype(BF)
    length = jnp.zeros((8, HD), jnp.int32) + blen[0]
    info = jnp.concatenate([length // 128, lax.rem(length, 128)], axis=0).astype(F32).astype(BF)
    sml[c, 0:16, :] = jnp.concatenate([qk[...].astype(F32), qv[...].astype(F32)], axis=0).astype(BF)
    sml[c, 16:32, :] = jnp.concatenate([key_pos, key_pos], axis=0).astype(BF)
    sml[c, 32:48, :] = info

    for copy in loads:
        copy.wait()
    pl.semaphore_wait(barrier, len(peers))

    for d in ZORDER:
        send(qbuf.at[z], qbuf.at[z], S_Q + d - 1, dev(c, at_z(d), t))
    first, second = pl.ds(0, 2), pl.ds(2, 1)
    for d in YORDER:
        send(kvb.at[c, first], kvb.at[c, first], S_KV + 2 * (d - 1), next_to(d))
    for d in YORDER:
        send(sml.at[c], sml.at[c], S_SM + d - 1, next_to(d))
    for d in YORDER:
        send(kvb.at[c, second], kvb.at[c, second], S_KV + 2 * (d - 1) + 1, next_to(d))

    root = ctx == 0

    @pl.when(root)
    def _():
        for j in range(NZ):
            for i in range(4):
                for q in range(SL // 16):
                    row = (i * NZ + (j - 1) % NZ if i == 2 else i * NZ + j) * SL + 16 * q
                    a, n, r = row // (2 * THIRD), row // THIRD % 2, row % THIRD
                    rst[j, i, 16 * q:16 * q + 16, :] = kvb[0, a, n, r:r + 16, :]
                rst[j, i, SL:SL + 16, :] = info
        ast[...] = rst[0]
        for j in range(1, NZ):
            remote(rst.at[j], ast, S_AA + j - 1, S_AA, dev(0, j, t)).start()

    row_of = lax.broadcasted_iota(jnp.int32, (THIRD, HD), 0)

    def live_keys(live, keys, other, values, to_kk, to_va, rows):
        to_kk[rows, :] = jnp.where(live, keys, other)
        to_va[rows, :HD] = jnp.where(live, values, jnp.zeros_like(values))
        to_va[rows, HD:] = jnp.where(live, 1.0, 0.0).astype(BF)

    for a in range(3):
        live_keys(
            row_of + a * THIRD < blen[0], kvb[c, a, 0], kvb[c, 0, 0, 0:1, :], kvb[c, a, 1],
            kk, va, slice(a * THIRD, (a + 1) * THIRD),
        )
    rr = lax.broadcasted_iota(jnp.int32, (TILE, TILE), 0)
    cc = lax.broadcasted_iota(jnp.int32, (TILE, TILE), 1)
    bias[...] = jnp.where(cc <= rr, 0.0, NEG)
    load_q.wait()

    def own_step(rb, h):
        qt = cqv[rb * TILE:(rb + 1) * TILE, pl.ds(pl.multiple_of(h * HD, HD), HD)]
        diagonal = slice(rb * TILE, (rb + 1) * TILE)
        sd = lax.dot_general(qt, kk[diagonal], NT, preferred_element_type=F32) + bias[...]
        top = jnp.max(sd, axis=1, keepdims=True)
        if rb:
            so = lax.dot_general(qt, kk[0:rb * TILE], NT, preferred_element_type=F32)
            top = jnp.maximum(top, jnp.max(so, axis=1, keepdims=True))
        top_s = top * SCALE
        pd = jnp.exp2(sd * SCALE - top_s).astype(BF)
        acc = jnp.dot(pd, va[diagonal], preferred_element_type=F32)
        if rb:
            po = jnp.exp2(so * SCALE - top_s).astype(BF)
            acc = acc + jnp.dot(po, va[0:rb * TILE], preferred_element_type=F32)
        acco[rb * HEADS + h] = acc
        mo[rb * HEADS + h] = jnp.broadcast_to(top_s, (TILE, HD))

    def own_steps(rb):
        @pl.loop(0, HEADS // HG)
        def _(i):
            for u in range(HG):
                own_step(rb, i * HG + u)

    own_steps(0)

    @pl.when(c == 0)
    def _():
        @pl.when(z != 0)
        def _():
            recv(ast, S_AA)
        akv[0, z] = ast[0]
        for d in range(1, NY):
            remote(ast.at[d], akv.at[d, z_to(d)], S_AB + d - 1, S_AB, next_to(d)).start()

    own_steps(1)

    @pl.when(c != 0)
    def _():
        recv(akv.at[c, z], S_AB)

    for d in ZORDER:
        send(akv.at[c, z], akv.at[c, z], S_AC + d - 1, dev(c, at_z(d), t))

    for d in range(1, NZ):
        recv(qbuf.at[at_z(-d)], S_Q + d - 1)
    for d in range(1, NY):
        recv(sml.at[at_c(-d)], S_SM + d - 1)
    half = NZ // 2 * 64

    def asked(i):
        return jnp.concatenate([qbuf[i * 4 + j, 0:64, :] for j in range(4)], axis=0)

    small = [sml[j].astype(F32) for j in range(NY)]
    zero96 = jnp.zeros((HD - NY * QROWS, HD), F32)
    ext_k = jnp.concatenate([s[0:8] for s in small] + [zero96], axis=0).astype(BF)
    ext_v = jnp.concatenate([s[8:16] for s in small] + [zero96], axis=0).astype(BF)
    ext_va = jnp.concatenate([ext_v, jnp.ones((HD, HD), BF)], axis=1)
    ext_pos = functools.reduce(jnp.minimum, [s[16:17] for s in small])

    for i in range(2):
        qt = asked(i)
        rows_pos = jnp.concatenate(
            [p for j in range(4) for p in [qbuf[i * 4 + j, 64:80, :].astype(F32)[0:8]] * HEADS], axis=0
        )
        se = lax.dot_general(qt, ext_k, NT, preferred_element_type=F32)
        se = jnp.where(ext_pos <= rows_pos, se, NEG)
        sa = lax.dot_general(qt, kk[...], NT, preferred_element_type=F32)
        top = jnp.maximum(jnp.max(se, axis=1, keepdims=True), jnp.max(sa, axis=1, keepdims=True)) * SCALE
        acc = jnp.dot(jnp.exp2(sa * SCALE - top).astype(BF), va[...], preferred_element_type=F32)
        acc = acc + jnp.dot(jnp.exp2(se * SCALE - top).astype(BF), ext_va, preferred_element_type=F32)
        m2[i * half:(i + 1) * half] = jnp.broadcast_to(top, (half, HD))
        acc2[i * half:(i + 1) * half] = acc

    def phase_two(thirds):
        at = 0
        for d in range(1, NY):
            slot = at_c(-d)
            length = sml[slot, 32:48, :].astype(F32)
            live_to = length[0:1] * 128.0 + length[8:9]
            for a in thirds:
                live_keys(
                    (row_of + a * THIRD).astype(F32) < live_to, kvb[slot, a, 0], kvb[slot, 0, 0, 0:1, :],
                    kvb[slot, a, 1], p2kk, p2va, slice(at, at + THIRD),
                )
                at += THIRD
        for i in range(2):
            part = slice(i * half, (i + 1) * half)
            sa = lax.dot_general(asked(i), p2kk[0:at], NT, preferred_element_type=F32)
            old = m2[part]
            top = jnp.maximum(jnp.max(sa, axis=1, keepdims=True) * SCALE, old)
            acc = jnp.dot(jnp.exp2(sa * SCALE - top[:, 0:1]).astype(BF), p2va[0:at], preferred_element_type=F32)
            keep = jnp.exp2(old - top)
            acc2[part] = acc + acc2[part] * jnp.concatenate([keep, keep], axis=1)
            m2[part] = top

    for d in range(1, NY):
        recv(kvb.at[at_c(-d), first], S_KV + 2 * (d - 1))
    phase_two((0, 1))
    for d in range(1, NY):
        recv(kvb.at[at_c(-d), second], S_KV + 2 * (d - 1) + 1)
    phase_two((2,))

    total = acc2[:, HD:]
    lse = m2[...] + jnp.log(total) * LOG2E
    part_out = acc2[:, :HD] / total
    for j in range(NZ):
        compact = jnp.zeros((8, HD), F32)
        for h in range(HEADS):
            compact = jnp.where(lane8 == h, lse[j * 64 + h * 8:j * 64 + h * 8 + 8], compact)
        high = compact.astype(BF).astype(F32)
        middle = (compact - high).astype(BF).astype(F32)
        low = compact - high - middle
        cmsg[j, 0:64, :] = part_out[j * 64:(j + 1) * 64].astype(BF)
        cmsg[j, 64:96, :] = jnp.concatenate([high, middle, low, jnp.zeros((8, HD), F32)], axis=0).astype(BF)
    for d in ZORDER:
        send(cmsg.at[at_z(d)], crecv.at[z], S_PZ + d - 1, dev(c, at_z(d), t))

    own_steps(2)

    for d in range(1, NZ):
        recv(akv.at[c, at_z(-d)], S_AC + d - 1)
    data = pl.ds(0, SL)
    for d in YORDER:
        send(akv.at[c, :, data], akv.at[c, :, data], S_AD + d - 1, next_to(d))

    for d in range(1, NZ):
        recv(crecv.at[at_z(-d)], S_PZ + d - 1)
    parts = [cmsg[z].astype(F32)] + [crecv[at_z(-d)].astype(F32) for d in range(1, NZ)]
    lses = [p[64:72] + p[72:80] + p[80:88] for p in parts]
    top = functools.reduce(jnp.maximum, lses)
    weights = [jnp.exp2(x - top) for x in lses]
    weight_sum = functools.reduce(jnp.add, weights)
    weights = [x / weight_sum for x in weights]
    merged = []
    for h in range(HEADS):
        merged.append(functools.reduce(
            jnp.add, [x[:, h:h + 1] * p[h * 8:h * 8 + 8] for x, p in zip(weights, parts)]
        ))
    merged = jnp.concatenate(
        [jnp.concatenate(merged[0:4], axis=1), jnp.concatenate(merged[4:8], axis=1)], axis=0
    )
    abuf[c, z] = merged.astype(BF)

    for d in ZORDER:
        send(abuf.at[c, z], abuf.at[c, z], S_TZ + d - 1, dev(c, at_z(d), t))

    def pass_on(k):
        zz = at_z(-k)
        if k:
            recv(abuf.at[c, zz], S_TZ + k - 1)
        for d in YORDER:
            send(abuf.at[c, zz], abuf.at[c, zz], S_TY + 3 * k + d - 1, next_to(d))

    pass_on(0)

    for d in range(1, NY):
        recv(akv.at[at_c(-d), :, data], S_AD + d - 1)
    alen = akv[c, z, SL:SL + 16, :].astype(F32)
    alive_to = jnp.where(ctx == 0, 0.0, alen[0:1] * 128.0 + alen[8:9])
    anchor = akv[:, :, 0:SL, :].reshape(2 * ROWS, HD)
    for a in range(3):
        keys_at = 2 * a * THIRD
        live_keys(
            (row_of + a * THIRD).astype(F32) < alive_to, anchor[keys_at:keys_at + THIRD], anchor[0:1],
            anchor[keys_at + THIRD:keys_at + 2 * THIRD], akk, ava, slice(a * THIRD, (a + 1) * THIRD),
        )

    def anchor_step(rb, h):
        cols = pl.ds(pl.multiple_of(h * HD, HD), HD)
        rows = slice(rb * TILE, (rb + 1) * TILE)
        sa = lax.dot_general(cqv[rows, cols], akk[...], NT, preferred_element_type=F32)
        old = mo[rb * HEADS + h]
        top = jnp.maximum(jnp.max(sa, axis=1, keepdims=True) * SCALE, old)
        acc = jnp.dot(jnp.exp2(sa * SCALE - top[:, 0:1]).astype(BF), ava[...], preferred_element_type=F32)
        keep = jnp.exp2(old - top)
        acc = acc + acco[rb * HEADS + h] * jnp.concatenate([keep, keep], axis=1)
        obuf[rows, cols] = (acc[:, :HD] / acc[:, HD:]).astype(BF)

    stores = [
        pltpu.make_async_copy(obuf.at[pl.ds(rb * TILE, TILE)], out.at[pl.ds(rb * TILE, TILE)], ls.at[rb])
        for rb in range(NRB)
    ]

    def anchor_steps(rb):
        @pl.loop(0, HEADS // HG)
        def _(i):
            for u in range(HG):
                anchor_step(rb, i * HG + u)

        stores[rb].start()

    anchor_steps(0)
    for k in ZORDER:
        pass_on(k)
    anchor_steps(1)
    load_w.wait()
    for k in range(NZ):
        for d in range(1, NY):
            recv(abuf.at[at_c(-d), lax.rem(z_from(d) - k + NZ, NZ)], S_TY + 3 * k + d - 1)

    rows = jnp.concatenate([abuf[(yy + 2 * zz) % NY, zz] for yy in range(NY) for zz in range(NZ)], axis=0)
    upper = jnp.dot(rows, wv[0:4 * HD], preferred_element_type=F32).reshape(NY * NZ, 16, -1)
    lower = jnp.dot(rows, wv[4 * HD:], preferred_element_type=F32).reshape(NY * NZ, 16, -1)
    partial = (upper[:, 0:8] + lower[:, 8:16]).reshape(pown.shape)
    pown[...] = partial
    psend[...] = partial.astype(BF)
    for d in range(1, TP):
        send(psend.at[at_t(d)], prec.at[t], S_RX + d - 1, dev(c, z, at_t(d)))
    anchor_steps(2)
    for d in range(1, TP):
        recv(prec.at[at_t(-d)], S_RX + d - 1)
    answer = pown[t]
    for d in range(1, TP):
        answer = answer + prec[at_t(-d)].astype(F32)
    ansb[t] = answer.astype(BF)
    for d in range(1, TP):
        send(ansb.at[t], ansb.at[t], S_GX + d - 1, dev(c, z, at_t(d)))
    for d in range(1, TP):
        recv(ansb.at[at_t(-d)], S_GX + d - 1)
    ans[...] = ansb[...].reshape(ans.shape)

    for copy in sends:
        copy.wait_send()

    @pl.when(root)
    def _():
        for j in range(1, NZ):
            remote(rst.at[j], ast, S_AA + j - 1, S_AA, dev(0, j, t)).wait_send()

    @pl.when(c == 0)
    def _():
        for d in range(1, NY):
            remote(ast.at[d], akv.at[d, z_to(d)], S_AB + d - 1, S_AB, next_to(d)).wait_send()

    for copy in stores:
        copy.wait()


def body(cq, ck, cv, blen, qq, qk, qv, qpos, w):
    hbm = pl.BlockSpec(memory_space=pl.ANY)
    vmem = pl.BlockSpec(memory_space=pltpu.VMEM)
    smem = pl.BlockSpec(memory_space=pltpu.SMEM)
    columns = w.shape[1]
    v = pltpu.VMEM
    return pl.pallas_call(
        kernel,
        out_shape=(
            jax.ShapeDtypeStruct(cq.shape, BF),
            jax.ShapeDtypeStruct((NY * NZ * QROWS, columns), BF),
        ),
        in_specs=[hbm, hbm, hbm, smem, hbm, hbm, hbm, smem, hbm],
        out_specs=(hbm, vmem),
        scratch_shapes=[
            v(qq.shape, BF),
            v(qk.shape, BF),
            v(qv.shape, BF),
            v(cq.shape, BF),
            v(w.shape, BF),
            v((NY, 3, 2, THIRD, HD), BF),
            v((ROWS, HD), BF),
            v((ROWS, 2 * HD), BF),
            v((ROWS, HD), BF),
            v((ROWS, 2 * HD), BF),
            v((TILE, TILE), F32),
            v((NRB * HEADS, TILE, HD), F32),
            v((NRB * HEADS, TILE, 2 * HD), F32),
            v(cq.shape, BF),
            v((NZ, 80, HD), BF),
            v((NY, 48, HD), BF),
            v((NZ, 4, SL + 16, HD), BF),
            v((4, SL + 16, HD), BF),
            v((4, NZ, SL + 16, HD), BF),
            v((2 * ROWS, HD), BF),
            v((2 * ROWS, 2 * HD), BF),
            v((NZ * 64, HD), F32),
            v((NZ * 64, 2 * HD), F32),
            v((NZ, 96, HD), BF),
            v((NZ, 96, HD), BF),
            v((NY, NZ, 16, 4 * HD), BF),
            v((TP, NY * NZ, columns), F32),
            v((TP, NY * NZ, columns), BF),
            v((TP, NY * NZ, columns), BF),
            v((TP, NY * NZ, columns), BF),
            pltpu.SemaphoreType.DMA((N_SEM,)),
            pltpu.SemaphoreType.DMA((N_SEM,)),
            pltpu.SemaphoreType.DMA((12,)),
        ],
        compiler_params=pltpu.CompilerParams(
            collective_id=1, has_side_effects=True, vmem_limit_bytes=63 * 2**20
        ),
        name="star_attention",
    )(cq, ck, cv, blen, qq, qk, qv, qpos, w)


def solution(mesh):
    in_specs = (
        P("ctx", "tp"),
        P("ctx", "tp"),
        P("ctx", "tp"),
        P("ctx"),
        P("ctx", "tp"),
        P("ctx", "tp"),
        P("ctx", "tp"),
        P("ctx"),
        P("tp", "ctx"),
    )
    out_specs = (P("ctx", "tp"), P(None, "ctx"))
    return jax.shard_map(body, mesh=mesh, in_specs=in_specs, out_specs=out_specs, check_vma=False)
```

time: 71.7 us -> 73.7 us (1.028)
  Pallas kernels: 61.2 us -> 68.8 us
  local copies, waits for them, and re-layouts: 8.83 us -> 3.36 us
    pallas_call x1, Pallas kernels: 61.2 us -> 68.8 us  [body(): pl.pallas_call(kernel, out_shape=(jax.ShapeDtypeStruct(cq.shape, BF), jax...]
    unnamed x18 -> x4, local copies, waits for them, and re-layouts: 8.83 us -> 3.36 us
where the time goes in v2:
time: 73.7 us; the launch traced here: 73.5 us
  Pallas kernels  68.8 us (93%)
  local copies, waits for them, and re-layouts  3.36 us (5%)
  between operations  1.29 us (2%)
    pallas_call x1, Pallas kernels, body(): pl.pallas_call(kernel, out_shape=(jax.ShapeDtypeStruct(cq.shape, BF), jax...  68.8 us
    unnamed x4, local copies, waits for them, and re-layouts  3.36 us

profile of v2, /device:TPU:1, one launch (start us, length us, event | category | flops | bytes accessed | tf_op | source)
XLA Modules:
  0.0 73.5 jit_solution(13299847909066778118)
XLA Ops:
  1.3 68.8 %star_attention.1 = (bf16[768,1024]{1,0:T(8,128)(2,1)}, bf16[256,256]{1,0:T(8,128)(2,1)}) custom-call(bf16[768,1024]{1,0:T(8,128)(2,1)} %cq.1, bf16[768,128]{1,0:T(8,128)(2,1)} %ck.1, bf16[768,128]{1,0:T(8,128)(2,1)} %cv.1, s32[1]{0:T(128)S(6)} %copy.13.blen, bf16[8,1024]{1,0:T(8,128)(2,1)} %qq_hbm.1, bf16[8,128]{1,0:T(8,128)(2,1)} %qk_hbm.1, ...), custom_call_target="tpu_custom_call" | custom-call | tf_op jit(solution)/shard_map/star_attention/pallas_call | solution.py:419
  70.1 0.0 copy-start
  70.1 2.7 %copy.14 = bf16[768,1024]{1,0:T(8,128)(2,1)} copy(bf16[768,1024]{1,0:T(8,128)(2,1)} %get-tuple-element.4) | data formatting | bytes 3145728
  72.8 0.0 copy-done
  72.8 0.7 copy.15
Async XLA Ops:
  70.1 2.7 %copy-start = (bf16[256,256]{1,0:T(8,128)(2,1)S(1)}, bf16[256,256]{1,0:T(8,128)(2,1)}, u32[]{:S(2)}) copy-start(bf16[256,256]{1,0:T(8,128)(2,1)} %get-tuple-element.5) | copy-start | bytes 393220

commit v3 on v2

--- a/solution.py
+++ b/solution.py
@@ -26,6 +26,7 @@
 LOG2E = math.log2(math.e)
 ZORDER = (1, 7, 2, 6, 3, 5, 4)
 YORDER = (1, 3, 2)
+COPIES = 4
 HG = 4
 
 S_Q, S_SM, S_KV, S_AA, S_AB, S_AC, S_AD = 0, 7, 10, 16, 23, 26, 33
@@ -197,23 +198,7 @@
 
     own_steps(0)
 
-    @pl.when(c == 0)
-    def _():
-        @pl.when(z != 0)
-        def _():
-            recv(ast, S_AA)
-        akv[0, z] = ast[0]
-        for d in range(1, NY):
-            remote(ast.at[d], akv.at[d, z_to(d)], S_AB + d - 1, S_AB, next_to(d)).start()
-
     own_steps(1)
-
-    @pl.when(c != 0)
-    def _():
-        recv(akv.at[c, z], S_AB)
-
-    for d in ZORDER:
-        send(akv.at[c, z], akv.at[c, z], S_AC + d - 1, dev(c, at_z(d), t))
 
     for d in range(1, NZ):
         recv(qbuf.at[at_z(-d)], S_Q + d - 1)
@@ -270,6 +255,15 @@
     for d in range(1, NY):
         recv(kvb.at[at_c(-d), first], S_KV + 2 * (d - 1))
     phase_two((0, 1))
+    @pl.when(c == 0)
+    def _():
+        @pl.when(z != 0)
+        def _():
+            recv(ast, S_AA)
+        akv[0, z] = ast[0]
+        for d in range(1, NY):
+            remote(ast.at[d], akv.at[d, z_to(d)], S_AB + d - 1, S_AB, next_to(d)).start()
+
     for d in range(1, NY):
         recv(kvb.at[at_c(-d), second], S_KV + 2 * (d - 1) + 1)
     phase_two((2,))
@@ -289,13 +283,14 @@
     for d in ZORDER:
         send(cmsg.at[at_z(d)], crecv.at[z], S_PZ + d - 1, dev(c, at_z(d), t))
 
+    @pl.when(c != 0)
+    def _():
+        recv(akv.at[c, z], S_AB)
+
+    for d in ZORDER:
+        send(akv.at[c, z], akv.at[c, z], S_AC + d - 1, dev(c, at_z(d), t))
+
     own_steps(2)
-
-    for d in range(1, NZ):
-        recv(akv.at[c, at_z(-d)], S_AC + d - 1)
-    data = pl.ds(0, SL)
-    for d in YORDER:
-        send(akv.at[c, :, data], akv.at[c, :, data], S_AD + d - 1, next_to(d))
 
     for d in range(1, NZ):
         recv(crecv.at[at_z(-d)], S_PZ + d - 1)
@@ -326,6 +321,14 @@
             send(abuf.at[c, zz], abuf.at[c, zz], S_TY + 3 * k + d - 1, next_to(d))
 
     pass_on(0)
+    for d in range(1, NZ):
+        recv(akv.at[c, at_z(-d)], S_AC + d - 1)
+    data = pl.ds(0, SL)
+    for d in YORDER:
+        send(akv.at[c, :, data], akv.at[c, :, data], S_AD + d - 1, next_to(d))
+
+    for k in ZORDER:
+        pass_on(k)
 
     for d in range(1, NY):
         recv(akv.at[at_c(-d), :, data], S_AD + d - 1)
@@ -364,9 +367,6 @@
         stores[rb].start()
 
     anchor_steps(0)
-    for k in ZORDER:
-        pass_on(k)
-    anchor_steps(1)
     load_w.wait()
     for k in range(NZ):
         for d in range(1, NY):
@@ -380,7 +380,7 @@
     psend[...] = partial.astype(BF)
     for d in range(1, TP):
         send(psend.at[at_t(d)], prec.at[t], S_RX + d - 1, dev(c, z, at_t(d)))
-    anchor_steps(2)
+    anchor_steps(1)
     for d in range(1, TP):
         recv(prec.at[at_t(-d)], S_RX + d - 1)
     answer = pown[t]
@@ -389,6 +389,7 @@
     ansb[t] = answer.astype(BF)
     for d in range(1, TP):
         send(ansb.at[t], ansb.at[t], S_GX + d - 1, dev(c, z, at_t(d)))
+    anchor_steps(2)
     for d in range(1, TP):
         recv(ansb.at[at_t(-d)], S_GX + d - 1)
     ans[...] = ansb[...].reshape(ans.shape)
@@ -406,6 +407,26 @@
         for d in range(1, NY):
             remote(ast.at[d], akv.at[d, z_to(d)], S_AB + d - 1, S_AB, next_to(d)).wait_send()
 
+    for copy in stores:
+        copy.wait()
+
+
+def finish(block, answer, block_out, answer_out, held, held_answer, sem):
+    rows = ROWS // COPIES
+    pieces = [(block, held, block_out, pl.ds(i * rows, rows)) for i in range(COPIES)]
+    pieces.append((answer, held_answer, answer_out, pl.ds(0, answer.shape[0])))
+    loads = [
+        pltpu.make_async_copy(src.at[at], here.at[at], sem.at[2 * i]) for i, (src, here, _, at) in enumerate(pieces)
+    ]
+    stores = [
+        pltpu.make_async_copy(here.at[at], dst.at[at], sem.at[2 * i + 1])
+        for i, (_, here, dst, at) in enumerate(pieces)
+    ]
+    for copy in loads:
+        copy.start()
+    for load, store in zip(loads, stores):
+        load.wait()
+        store.start()
     for copy in stores:
         copy.wait()
 
@@ -416,7 +437,7 @@
     smem = pl.BlockSpec(memory_space=pltpu.SMEM)
     columns = w.shape[1]
     v = pltpu.VMEM
-    return pl.pallas_call(
+    results = pl.pallas_call(
         kernel,
         out_shape=(
             jax.ShapeDtypeStruct(cq.shape, BF),
@@ -464,6 +485,15 @@
         ),
         name="star_attention",
     )(cq, ck, cv, blen, qq, qk, qv, qpos, w)
+    return pl.pallas_call(
+        finish,
+        out_shape=tuple(jax.ShapeDtypeStruct(x.shape, x.dtype) for x in results),
+        in_specs=[hbm, hbm],
+        out_specs=(hbm, hbm),
+        scratch_shapes=[v(x.shape, x.dtype) for x in results] + [pltpu.SemaphoreType.DMA((2 * COPIES + 2,))],
+        compiler_params=pltpu.CompilerParams(vmem_limit_bytes=62 * 2**20),
+        name="results",
+    )(*results)
 
 
 def solution(mesh):

time: 73.7 us -> 68 us (0.923)
  local copies, waits for them, and re-layouts: 3.36 us -> 0 us
  Pallas kernels: 68.8 us -> 66.3 us
    pallas_call x1, Pallas kernels: 68.8 us -> 64.1 us  [body(): pl.pallas_call(kernel, out_shape=(jax.ShapeDtypeStruct(cq.shape, BF), jax...]
    unnamed x4 -> x0, local copies, waits for them, and re-layouts: 3.36 us -> none
    pallas_call x0 -> x1, Pallas kernels: none -> 2.26 us  [body(): pl.pallas_call(finish, out_shape=tuple((jax.ShapeDtypeStruct(x.shape, x.d...]
where the time goes in v3:
time: 68 us; the launch traced here: 67.8 us
  Pallas kernels  66.3 us (98%)
  between operations  1.45 us (2%)
    pallas_call x1, Pallas kernels, body(): pl.pallas_call(kernel, out_shape=(jax.ShapeDtypeStruct(cq.shape, BF), jax...  64.1 us
    pallas_call x1, Pallas kernels, body(): pl.pallas_call(finish, out_shape=tuple((jax.ShapeDtypeStruct(x.shape, x.d...  2.26 us

profile of v3, /device:TPU:1, one launch (start us, length us, event | category | flops | bytes accessed | tf_op | source)
XLA Modules:
  0.0 67.8 jit_solution(13408393252650174913)
XLA Ops:
  1.3 64.1 %star_attention.1 = (bf16[768,1024]{1,0:T(8,128)(2,1)}, bf16[256,256]{1,0:T(8,128)(2,1)}) custom-call(bf16[768,1024]{1,0:T(8,128)(2,1)} %cq.1, bf16[768,128]{1,0:T(8,128)(2,1)} %ck.1, bf16[768,128]{1,0:T(8,128)(2,1)} %cv.1, s32[1]{0:T(128)S(6)} %copy.11.blen, bf16[8,1024]{1,0:T(8,128)(2,1)} %qq_hbm.1, bf16[8,128]{1,0:T(8,128)(2,1)} %qk_hbm.1, ...), custom_call_target="tpu_custom_call" | custom-call | tf_op jit(solution)/shard_map/star_attention/pallas_call | solution.py:440
  65.3 2.3 %results.1 = (bf16[768,1024]{1,0:T(8,128)(2,1)}, bf16[256,256]{1,0:T(8,128)(2,1)}) custom-call(bf16[768,1024]{1,0:T(8,128)(2,1)} %get-tuple-element.4.block, bf16[256,256]{1,0:T(8,128)(2,1)} %get-tuple-element.5.answer), custom_call_target="tpu_custom_call" | custom-call | tf_op jit(solution)/shard_map/results/pallas_call | solution.py:488

commit v4 on v3

--- a/solution.py
+++ b/solution.py
@@ -29,9 +29,9 @@
 COPIES = 4
 HG = 4
 
-S_Q, S_SM, S_KV, S_AA, S_AB, S_AC, S_AD = 0, 7, 10, 16, 23, 26, 33
-S_PZ, S_TZ, S_TY, S_RX, S_GX = 36, 43, 50, 74, 81
-N_SEM = 88
+S_Q, S_SM, S_KV, S_AA, S_AB, S_AC, S_AD = 0, 7, 10, 22, 29, 32, 39
+S_PZ, S_TZ, S_TY, S_RX, S_GX = 42, 49, 56, 80, 87
+N_SEM = 94
 
 
 def kernel(
@@ -99,13 +99,22 @@
         for n, (src, dst) in enumerate(((qq_hbm, qq), (qk_hbm, qk), (qv_hbm, qv)))
     ]
     loads = [
-        pltpu.make_async_copy(src.at[pl.ds(a * THIRD, THIRD)], kvb.at[c, a, n], ls.at[3 + 2 * a + n])
-        for a in range(3) for n, src in enumerate((ck, cv))
+        pltpu.make_async_copy(src, kvb.at[c, n], ls.at[3 + n]) for n, src in enumerate((ck, cv))
     ]
-    load_q = pltpu.make_async_copy(cq, cqv, ls.at[9])
-    load_w = pltpu.make_async_copy(w, wv, ls.at[10])
+    load_q = pltpu.make_async_copy(cq, cqv, ls.at[5])
+    load_w = pltpu.make_async_copy(w, wv, ls.at[6])
     for copy in small_loads + loads + [load_q, load_w]:
         copy.start()
+    pl.semaphore_wait(barrier, len(peers))
+
+    first, second = pl.ds(0, 2 * THIRD), pl.ds(2 * THIRD, THIRD)
+
+    def send_keys(part, at):
+        for d in YORDER:
+            for n, src in enumerate((ck, cv)):
+                send(src.at[at], kvb.at[c, n, at], S_KV + 4 * (d - 1) + 2 * part + n, next_to(d))
+
+    send_keys(0, first)
     for copy in small_loads:
         copy.wait()
 
@@ -127,19 +136,13 @@
     sml[c, 16:32, :] = jnp.concatenate([key_pos, key_pos], axis=0).astype(BF)
     sml[c, 32:48, :] = info
 
+    for d in ZORDER:
+        send(qbuf.at[z], qbuf.at[z], S_Q + d - 1, dev(c, at_z(d), t))
+    for d in YORDER:
+        send(sml.at[c], sml.at[c], S_SM + d - 1, next_to(d))
+    send_keys(1, second)
     for copy in loads:
         copy.wait()
-    pl.semaphore_wait(barrier, len(peers))
-
-    for d in ZORDER:
-        send(qbuf.at[z], qbuf.at[z], S_Q + d - 1, dev(c, at_z(d), t))
-    first, second = pl.ds(0, 2), pl.ds(2, 1)
-    for d in YORDER:
-        send(kvb.at[c, first], kvb.at[c, first], S_KV + 2 * (d - 1), next_to(d))
-    for d in YORDER:
-        send(sml.at[c], sml.at[c], S_SM + d - 1, next_to(d))
-    for d in YORDER:
-        send(kvb.at[c, second], kvb.at[c, second], S_KV + 2 * (d - 1) + 1, next_to(d))
 
     root = ctx == 0
 
@@ -147,10 +150,8 @@
     def _():
         for j in range(NZ):
             for i in range(4):
-                for q in range(SL // 16):
-                    row = (i * NZ + (j - 1) % NZ if i == 2 else i * NZ + j) * SL + 16 * q
-                    a, n, r = row // (2 * THIRD), row // THIRD % 2, row % THIRD
-                    rst[j, i, 16 * q:16 * q + 16, :] = kvb[0, a, n, r:r + 16, :]
+                n, row = divmod((i * NZ + (j - 1) % NZ if i == 2 else i * NZ + j) * SL, ROWS)
+                rst[j, i, 0:SL, :] = kvb[0, n, row:row + SL, :]
                 rst[j, i, SL:SL + 16, :] = info
         ast[...] = rst[0]
         for j in range(1, NZ):
@@ -165,8 +166,8 @@
 
     for a in range(3):
         live_keys(
-            row_of + a * THIRD < blen[0], kvb[c, a, 0], kvb[c, 0, 0, 0:1, :], kvb[c, a, 1],
-            kk, va, slice(a * THIRD, (a + 1) * THIRD),
+            row_of + a * THIRD < blen[0], kvb[c, 0, a * THIRD:(a + 1) * THIRD], kvb[c, 0, 0:1],
+            kvb[c, 1, a * THIRD:(a + 1) * THIRD], kk, va, slice(a * THIRD, (a + 1) * THIRD),
         )
     rr = lax.broadcasted_iota(jnp.int32, (TILE, TILE), 0)
     cc = lax.broadcasted_iota(jnp.int32, (TILE, TILE), 1)
@@ -199,6 +200,7 @@
     own_steps(0)
 
     own_steps(1)
+    own_steps(2)
 
     for d in range(1, NZ):
         recv(qbuf.at[at_z(-d)], S_Q + d - 1)
@@ -238,8 +240,8 @@
             live_to = length[0:1] * 128.0 + length[8:9]
             for a in thirds:
                 live_keys(
-                    (row_of + a * THIRD).astype(F32) < live_to, kvb[slot, a, 0], kvb[slot, 0, 0, 0:1, :],
-                    kvb[slot, a, 1], p2kk, p2va, slice(at, at + THIRD),
+                    (row_of + a * THIRD).astype(F32) < live_to, kvb[slot, 0, a * THIRD:(a + 1) * THIRD],
+                    kvb[slot, 0, 0:1], kvb[slot, 1, a * THIRD:(a + 1) * THIRD], p2kk, p2va, slice(at, at + THIRD),
                 )
                 at += THIRD
         for i in range(2):
@@ -252,20 +254,14 @@
             acc2[part] = acc + acc2[part] * jnp.concatenate([keep, keep], axis=1)
             m2[part] = top
 
-    for d in range(1, NY):
-        recv(kvb.at[at_c(-d), first], S_KV + 2 * (d - 1))
+    def recv_keys(part, at):
+        for d in range(1, NY):
+            for n in range(2):
+                recv(kvb.at[at_c(-d), n, at], S_KV + 4 * (d - 1) + 2 * part + n)
+
+    recv_keys(0, first)
     phase_two((0, 1))
-    @pl.when(c == 0)
-    def _():
-        @pl.when(z != 0)
-        def _():
-            recv(ast, S_AA)
-        akv[0, z] = ast[0]
-        for d in range(1, NY):
-            remote(ast.at[d], akv.at[d, z_to(d)], S_AB + d - 1, S_AB, next_to(d)).start()
-
-    for d in range(1, NY):
-        recv(kvb.at[at_c(-d), second], S_KV + 2 * (d - 1) + 1)
+    recv_keys(1, second)
     phase_two((2,))
 
     total = acc2[:, HD:]
@@ -283,6 +279,15 @@
     for d in ZORDER:
         send(cmsg.at[at_z(d)], crecv.at[z], S_PZ + d - 1, dev(c, at_z(d), t))
 
+    @pl.when(c == 0)
+    def _():
+        @pl.when(z != 0)
+        def _():
+            recv(ast, S_AA)
+        akv[0, z] = ast[0]
+        for d in range(1, NY):
+            remote(ast.at[d], akv.at[d, z_to(d)], S_AB + d - 1, S_AB, next_to(d)).start()
+
     @pl.when(c != 0)
     def _():
         recv(akv.at[c, z], S_AB)
@@ -290,7 +295,6 @@
     for d in ZORDER:
         send(akv.at[c, z], akv.at[c, z], S_AC + d - 1, dev(c, at_z(d), t))
 
-    own_steps(2)
 
     for d in range(1, NZ):
         recv(crecv.at[at_z(-d)], S_PZ + d - 1)
@@ -330,18 +334,6 @@
     for k in ZORDER:
         pass_on(k)
 
-    for d in range(1, NY):
-        recv(akv.at[at_c(-d), :, data], S_AD + d - 1)
-    alen = akv[c, z, SL:SL + 16, :].astype(F32)
-    alive_to = jnp.where(ctx == 0, 0.0, alen[0:1] * 128.0 + alen[8:9])
-    anchor = akv[:, :, 0:SL, :].reshape(2 * ROWS, HD)
-    for a in range(3):
-        keys_at = 2 * a * THIRD
-        live_keys(
-            (row_of + a * THIRD).astype(F32) < alive_to, anchor[keys_at:keys_at + THIRD], anchor[0:1],
-            anchor[keys_at + THIRD:keys_at + 2 * THIRD], akk, ava, slice(a * THIRD, (a + 1) * THIRD),
-        )
-
     def anchor_step(rb, h):
         cols = pl.ds(pl.multiple_of(h * HD, HD), HD)
         rows = slice(rb * TILE, (rb + 1) * TILE)
@@ -366,7 +358,6 @@
 
         stores[rb].start()
 
-    anchor_steps(0)
     load_w.wait()
     for k in range(NZ):
         for d in range(1, NY):
@@ -380,6 +371,19 @@
     psend[...] = partial.astype(BF)
     for d in range(1, TP):
         send(psend.at[at_t(d)], prec.at[t], S_RX + d - 1, dev(c, z, at_t(d)))
+    for d in range(1, NY):
+        recv(akv.at[at_c(-d), :, data], S_AD + d - 1)
+    alen = akv[c, z, SL:SL + 16, :].astype(F32)
+    alive_to = jnp.where(ctx == 0, 0.0, alen[0:1] * 128.0 + alen[8:9])
+    anchor = akv[:, :, 0:SL, :].reshape(2 * ROWS, HD)
+    for a in range(3):
+        keys_at = a * THIRD
+        live_keys(
+            (row_of + a * THIRD).astype(F32) < alive_to, anchor[keys_at:keys_at + THIRD], anchor[0:1],
+            anchor[ROWS + keys_at:ROWS + keys_at + THIRD], akk, ava, slice(a * THIRD, (a + 1) * THIRD),
+        )
+
+    anchor_steps(0)
     anchor_steps(1)
     for d in range(1, TP):
         recv(prec.at[at_t(-d)], S_RX + d - 1)
@@ -451,7 +455,7 @@
             v(qv.shape, BF),
             v(cq.shape, BF),
             v(w.shape, BF),
-            v((NY, 3, 2, THIRD, HD), BF),
+            v((NY, 2, ROWS, HD), BF),
             v((ROWS, HD), BF),
             v((ROWS, 2 * HD), BF),
             v((ROWS, HD), BF),

time: 68 us -> 67.8 us (level)
  no operation moved by 1% of the time
where the time goes in v4:
time: 67.8 us; the launch traced here: 67.6 us
  Pallas kernels  66.2 us (98%)
  between operations  1.45 us (2%)
    pallas_call x1, Pallas kernels, body(): pl.pallas_call(kernel, out_shape=(jax.ShapeDtypeStruct(cq.shape, BF), jax...  63.9 us
    pallas_call x1, Pallas kernels, body(): pl.pallas_call(finish, out_shape=tuple((jax.ShapeDtypeStruct(x.shape, x.d...  2.26 us

profile of v4, /device:TPU:1, one launch (start us, length us, event | category | flops | bytes accessed | tf_op | source)
XLA Modules:
  0.0 67.6 jit_solution(5006749648602408137)
XLA Ops:
  1.3 63.9 %star_attention.1 = (bf16[768,1024]{1,0:T(8,128)(2,1)}, bf16[256,256]{1,0:T(8,128)(2,1)}) custom-call(bf16[768,1024]{1,0:T(8,128)(2,1)} %cq.1, bf16[768,128]{1,0:T(8,128)(2,1)} %ck.1, bf16[768,128]{1,0:T(8,128)(2,1)} %cv.1, s32[1]{0:T(128)S(6)} %copy.11.blen, bf16[8,1024]{1,0:T(8,128)(2,1)} %qq_hbm.1, bf16[8,128]{1,0:T(8,128)(2,1)} %qk_hbm.1, ...), custom_call_target="tpu_custom_call" | custom-call | tf_op jit(solution)/shard_map/star_attention/pallas_call | solution.py:444
  65.2 2.3 %results.1 = (bf16[768,1024]{1,0:T(8,128)(2,1)}, bf16[256,256]{1,0:T(8,128)(2,1)}) custom-call(bf16[768,1024]{1,0:T(8,128)(2,1)} %get-tuple-element.4.block, bf16[256,256]{1,0:T(8,128)(2,1)} %get-tuple-element.5.answer), custom_call_target="tpu_custom_call" | custom-call | tf_op jit(solution)/shard_map/results/pallas_call | solution.py:492

commit v5 on v4

--- a/solution.py
+++ b/solution.py
@@ -29,9 +29,9 @@
 COPIES = 4
 HG = 4
 
-S_Q, S_SM, S_KV, S_AA, S_AB, S_AC, S_AD = 0, 7, 10, 22, 29, 32, 39
-S_PZ, S_TZ, S_TY, S_RX, S_GX = 42, 49, 56, 80, 87
-N_SEM = 94
+S_Q, S_SM, S_KV, S_AA, S_AC, S_AD = 0, 7, 10, 22, 29, 36
+S_PZ, S_TZ, S_TY, S_RX, S_GX = 39, 46, 53, 77, 84
+N_SEM = 91
 
 
 def kernel(
@@ -39,7 +39,7 @@
     out, ans,
     qq, qk, qv, cqv, wv, kvb, kk, va, akk, ava, bias,
     mo, acco, obuf,
-    qbuf, sml, rst, ast, akv,
+    qbuf, sml, rst, akv,
     p2kk, p2va, m2, acc2,
     cmsg, crecv, abuf, pown, psend, prec, ansb,
     ss, rs, ls,
@@ -143,19 +143,6 @@
     send_keys(1, second)
     for copy in loads:
         copy.wait()
-
-    root = ctx == 0
-
-    @pl.when(root)
-    def _():
-        for j in range(NZ):
-            for i in range(4):
-                n, row = divmod((i * NZ + (j - 1) % NZ if i == 2 else i * NZ + j) * SL, ROWS)
-                rst[j, i, 0:SL, :] = kvb[0, n, row:row + SL, :]
-                rst[j, i, SL:SL + 16, :] = info
-        ast[...] = rst[0]
-        for j in range(1, NZ):
-            remote(rst.at[j], ast, S_AA + j - 1, S_AA, dev(0, j, t)).start()
 
     row_of = lax.broadcasted_iota(jnp.int32, (THIRD, HD), 0)
 
@@ -262,6 +249,20 @@
     recv_keys(0, first)
     phase_two((0, 1))
     recv_keys(1, second)
+
+    source_z = jnp.where(c == 2, NZ - 1, 0)
+
+    @pl.when(z == source_z)
+    def _():
+        for j in range(NZ):
+            row = pl.multiple_of(lax.rem(c, 2) * (ROWS // 2) + j * SL, 16)
+            rst[j, 0:SL, :] = kvb[0, c // 2, pl.ds(row, SL), :]
+            rst[j, SL:SL + 16, :] = sml[0, 32:48, :]
+        akv[c, z] = rst[z]
+        for d in range(1, NZ):
+            to_z = at_z(d)
+            remote(rst.at[to_z], akv.at[c, to_z], S_AA + d - 1, S_AA, dev(c, to_z, t)).start()
+
     phase_two((2,))
 
     total = acc2[:, HD:]
@@ -279,18 +280,9 @@
     for d in ZORDER:
         send(cmsg.at[at_z(d)], crecv.at[z], S_PZ + d - 1, dev(c, at_z(d), t))
 
-    @pl.when(c == 0)
+    @pl.when(z != source_z)
     def _():
-        @pl.when(z != 0)
-        def _():
-            recv(ast, S_AA)
-        akv[0, z] = ast[0]
-        for d in range(1, NY):
-            remote(ast.at[d], akv.at[d, z_to(d)], S_AB + d - 1, S_AB, next_to(d)).start()
-
-    @pl.when(c != 0)
-    def _():
-        recv(akv.at[c, z], S_AB)
+        recv(akv.at[c, z], S_AA)
 
     for d in ZORDER:
         send(akv.at[c, z], akv.at[c, z], S_AC + d - 1, dev(c, at_z(d), t))
@@ -358,19 +350,6 @@
 
         stores[rb].start()
 
-    load_w.wait()
-    for k in range(NZ):
-        for d in range(1, NY):
-            recv(abuf.at[at_c(-d), lax.rem(z_from(d) - k + NZ, NZ)], S_TY + 3 * k + d - 1)
-
-    rows = jnp.concatenate([abuf[(yy + 2 * zz) % NY, zz] for yy in range(NY) for zz in range(NZ)], axis=0)
-    upper = jnp.dot(rows, wv[0:4 * HD], preferred_element_type=F32).reshape(NY * NZ, 16, -1)
-    lower = jnp.dot(rows, wv[4 * HD:], preferred_element_type=F32).reshape(NY * NZ, 16, -1)
-    partial = (upper[:, 0:8] + lower[:, 8:16]).reshape(pown.shape)
-    pown[...] = partial
-    psend[...] = partial.astype(BF)
-    for d in range(1, TP):
-        send(psend.at[at_t(d)], prec.at[t], S_RX + d - 1, dev(c, z, at_t(d)))
     for d in range(1, NY):
         recv(akv.at[at_c(-d), :, data], S_AD + d - 1)
     alen = akv[c, z, SL:SL + 16, :].astype(F32)
@@ -384,6 +363,19 @@
         )
 
     anchor_steps(0)
+    load_w.wait()
+    for k in range(NZ):
+        for d in range(1, NY):
+            recv(abuf.at[at_c(-d), lax.rem(z_from(d) - k + NZ, NZ)], S_TY + 3 * k + d - 1)
+
+    rows = jnp.concatenate([abuf[(yy + 2 * zz) % NY, zz] for yy in range(NY) for zz in range(NZ)], axis=0)
+    upper = jnp.dot(rows, wv[0:4 * HD], preferred_element_type=F32).reshape(NY * NZ, 16, -1)
+    lower = jnp.dot(rows, wv[4 * HD:], preferred_element_type=F32).reshape(NY * NZ, 16, -1)
+    partial = (upper[:, 0:8] + lower[:, 8:16]).reshape(pown.shape)
+    pown[...] = partial
+    psend[...] = partial.astype(BF)
+    for d in range(1, TP):
+        send(psend.at[at_t(d)], prec.at[t], S_RX + d - 1, dev(c, z, at_t(d)))
     anchor_steps(1)
     for d in range(1, TP):
         recv(prec.at[at_t(-d)], S_RX + d - 1)
@@ -401,15 +393,11 @@
     for copy in sends:
         copy.wait_send()
 
-    @pl.when(root)
+    @pl.when(z == source_z)
     def _():
-        for j in range(1, NZ):
-            remote(rst.at[j], ast, S_AA + j - 1, S_AA, dev(0, j, t)).wait_send()
-
-    @pl.when(c == 0)
-    def _():
-        for d in range(1, NY):
-            remote(ast.at[d], akv.at[d, z_to(d)], S_AB + d - 1, S_AB, next_to(d)).wait_send()
+        for d in range(1, NZ):
+            to_z = at_z(d)
+            remote(rst.at[to_z], akv.at[c, to_z], S_AA + d - 1, S_AA, dev(c, to_z, t)).wait_send()
 
     for copy in stores:
         copy.wait()
@@ -466,8 +454,7 @@
             v(cq.shape, BF),
             v((NZ, 80, HD), BF),
             v((NY, 48, HD), BF),
-            v((NZ, 4, SL + 16, HD), BF),
-            v((4, SL + 16, HD), BF),
+            v((NZ, SL + 16, HD), BF),
             v((4, NZ, SL + 16, HD), BF),
             v((2 * ROWS, HD), BF),
             v((2 * ROWS, 2 * HD), BF),

time: 67.8 us -> 64.1 us (0.945)
  Pallas kernels: 66.2 us -> 62.5 us
    pallas_call x1, Pallas kernels: 63.9 us -> 60.3 us  [body(): pl.pallas_call(kernel, out_shape=(jax.ShapeDtypeStruct(cq.shape, BF), jax...]
where the time goes in v5:
time: 64.1 us; the launch traced here: 64 us
  Pallas kernels  62.5 us (98%)
  between operations  1.45 us (2%)
    pallas_call x1, Pallas kernels, body(): pl.pallas_call(kernel, out_shape=(jax.ShapeDtypeStruct(cq.shape, BF), jax...  60.3 us
    pallas_call x1, Pallas kernels, body(): pl.pallas_call(finish, out_shape=tuple((jax.ShapeDtypeStruct(x.shape, x.d...  2.26 us

profile of v5, /device:TPU:1, one launch (start us, length us, event | category | flops | bytes accessed | tf_op | source)
XLA Modules:
  0.0 64.0 jit_solution(13313075159423255598)
XLA Ops:
  1.3 60.3 %star_attention.1 = (bf16[768,1024]{1,0:T(8,128)(2,1)}, bf16[256,256]{1,0:T(8,128)(2,1)}) custom-call(bf16[768,1024]{1,0:T(8,128)(2,1)} %cq.1, bf16[768,128]{1,0:T(8,128)(2,1)} %ck.1, bf16[768,128]{1,0:T(8,128)(2,1)} %cv.1, s32[1]{0:T(128)S(6)} %copy.11.blen, bf16[8,1024]{1,0:T(8,128)(2,1)} %qq_hbm.1, bf16[8,128]{1,0:T(8,128)(2,1)} %qk_hbm.1, ...), custom_call_target="tpu_custom_call" | custom-call | tf_op jit(solution)/shard_map/star_attention/pallas_call | solution.py:432
  61.5 2.3 %results.1 = (bf16[768,1024]{1,0:T(8,128)(2,1)}, bf16[256,256]{1,0:T(8,128)(2,1)}) custom-call(bf16[768,1024]{1,0:T(8,128)(2,1)} %get-tuple-element.4.block, bf16[256,256]{1,0:T(8,128)(2,1)} %get-tuple-element.5.answer), custom_call_target="tpu_custom_call" | custom-call | tf_op jit(solution)/shard_map/results/pallas_call | solution.py:479

commit v6 on v5

--- a/solution.py
+++ b/solution.py
@@ -29,9 +29,9 @@
 COPIES = 4
 HG = 4
 
-S_Q, S_SM, S_KV, S_AA, S_AC, S_AD = 0, 7, 10, 22, 29, 36
-S_PZ, S_TZ, S_TY, S_RX, S_GX = 39, 46, 53, 77, 84
-N_SEM = 91
+S_Q, S_SM, S_KV, S_AA, S_AC, S_AD = 0, 7, 11, 27, 34, 41
+S_PZ, S_TZ, S_TY, S_RX, S_GX = 44, 51, 58, 82, 89
+N_SEM = 96
 
 
 def kernel(
@@ -107,14 +107,22 @@
         copy.start()
     pl.semaphore_wait(barrier, len(peers))
 
-    first, second = pl.ds(0, 2 * THIRD), pl.ds(2 * THIRD, THIRD)
-
-    def send_keys(part, at):
-        for d in YORDER:
-            for n, src in enumerate((ck, cv)):
-                send(src.at[at], kvb.at[c, n, at], S_KV + 4 * (d - 1) + 2 * part + n, next_to(d))
-
-    send_keys(0, first)
+    def key_parts(part):
+        at, length = (0, 2 * THIRD) if part == 0 else (2 * THIRD, THIRD)
+        whole, half = pl.ds(at, length), length // 2
+        return (
+            (whole, dev(at_c(1), z, t), at_c(-1)),
+            (whole, dev(at_c(3), z, t), at_c(-3)),
+            (pl.ds(at, half), dev(at_c(2), at_z(-1), t), at_c(2)),
+            (pl.ds(at + half, half), dev(at_c(2), at_z(1), t), at_c(2)),
+        )
+
+    def send_keys(part):
+        for n, src in enumerate((ck, cv)):
+            for k, (rows, peer, _) in enumerate(key_parts(part)):
+                send(src.at[rows], kvb.at[c, n, rows], S_KV + 8 * part + 4 * n + k, peer)
+
+    send_keys(0)
     for copy in small_loads:
         copy.wait()
 
@@ -140,7 +148,8 @@
         send(qbuf.at[z], qbuf.at[z], S_Q + d - 1, dev(c, at_z(d), t))
     for d in YORDER:
         send(sml.at[c], sml.at[c], S_SM + d - 1, next_to(d))
-    send_keys(1, second)
+    send(sml.at[c], sml.at[NY], S_SM + 3, dev(at_c(2), at_z(1), t))
+    send_keys(1)
     for copy in loads:
         copy.wait()
 
@@ -193,6 +202,7 @@
         recv(qbuf.at[at_z(-d)], S_Q + d - 1)
     for d in range(1, NY):
         recv(sml.at[at_c(-d)], S_SM + d - 1)
+    recv(sml.at[NY], S_SM + 3)
     half = NZ // 2 * 64
 
     def asked(i):
@@ -219,13 +229,20 @@
         m2[i * half:(i + 1) * half] = jnp.broadcast_to(top, (half, HD))
         acc2[i * half:(i + 1) * half] = acc
 
+    def length_of(slot):
+        length = sml[slot, 32:48, :].astype(F32)
+        return length[0:1] * 128.0 + length[8:9]
+
     def phase_two(thirds):
         at = 0
+        below = length_of(NY)
         for d in range(1, NY):
             slot = at_c(-d)
-            length = sml[slot, 32:48, :].astype(F32)
-            live_to = length[0:1] * 128.0 + length[8:9]
+            above = length_of(slot)
             for a in thirds:
+                live_to = above
+                if d == 2 and a:
+                    live_to = jnp.where(row_of < THIRD // 2, above, below) if a == 2 else below
                 live_keys(
                     (row_of + a * THIRD).astype(F32) < live_to, kvb[slot, 0, a * THIRD:(a + 1) * THIRD],
                     kvb[slot, 0, 0:1], kvb[slot, 1, a * THIRD:(a + 1) * THIRD], p2kk, p2va, slice(at, at + THIRD),
@@ -241,22 +258,22 @@
             acc2[part] = acc + acc2[part] * jnp.concatenate([keep, keep], axis=1)
             m2[part] = top
 
-    def recv_keys(part, at):
-        for d in range(1, NY):
-            for n in range(2):
-                recv(kvb.at[at_c(-d), n, at], S_KV + 4 * (d - 1) + 2 * part + n)
-
-    recv_keys(0, first)
+    def recv_keys(part):
+        for n in range(2):
+            for k, (rows, _, slot) in enumerate(key_parts(part)):
+                recv(kvb.at[slot, n, rows], S_KV + 8 * part + 4 * n + k)
+
+    recv_keys(0)
     phase_two((0, 1))
-    recv_keys(1, second)
+    recv_keys(1)
 
     source_z = jnp.where(c == 2, NZ - 1, 0)
 
     @pl.when(z == source_z)
     def _():
         for j in range(NZ):
-            row = pl.multiple_of(lax.rem(c, 2) * (ROWS // 2) + j * SL, 16)
-            rst[j, 0:SL, :] = kvb[0, c // 2, pl.ds(row, SL), :]
+            row = pl.multiple_of(at_c(2) * (ROWS // 4) + j % 4 * SL, 16)
+            rst[j, 0:SL, :] = kvb[0, j // 4, pl.ds(row, SL), :]
             rst[j, SL:SL + 16, :] = sml[0, 32:48, :]
         akv[c, z] = rst[z]
         for d in range(1, NZ):
@@ -276,7 +293,8 @@
         middle = (compact - high).astype(BF).astype(F32)
         low = compact - high - middle
         cmsg[j, 0:64, :] = part_out[j * 64:(j + 1) * 64].astype(BF)
-        cmsg[j, 64:96, :] = jnp.concatenate([high, middle, low, jnp.zeros((8, HD), F32)], axis=0).astype(BF)
+        pieces = high + pltpu.roll(middle, 8, 1) + pltpu.roll(low, 16, 1)
+        cmsg[j, 64:80, :] = jnp.concatenate([pieces, pieces], axis=0).astype(BF)
     for d in ZORDER:
         send(cmsg.at[at_z(d)], crecv.at[z], S_PZ + d - 1, dev(c, at_z(d), t))
 
@@ -291,7 +309,7 @@
     for d in range(1, NZ):
         recv(crecv.at[at_z(-d)], S_PZ + d - 1)
     parts = [cmsg[z].astype(F32)] + [crecv[at_z(-d)].astype(F32) for d in range(1, NZ)]
-    lses = [p[64:72] + p[72:80] + p[80:88] for p in parts]
+    lses = [p[64:72] + pltpu.roll(p[64:72], HD - 8, 1) + pltpu.roll(p[64:72], HD - 16, 1) for p in parts]
     top = functools.reduce(jnp.maximum, lses)
     weights = [jnp.exp2(x - top) for x in lses]
     weight_sum = functools.reduce(jnp.add, weights)
@@ -326,15 +344,15 @@
     for k in ZORDER:
         pass_on(k)
 
-    def anchor_step(rb, h):
-        cols = pl.ds(pl.multiple_of(h * HD, HD), HD)
-        rows = slice(rb * TILE, (rb + 1) * TILE)
+    def anchor_step(i):
+        cols = pl.ds(pl.multiple_of(lax.rem(i, HEADS) * HD, HD), HD)
+        rows = pl.ds(pl.multiple_of(i // HEADS * TILE, TILE), TILE)
         sa = lax.dot_general(cqv[rows, cols], akk[...], NT, preferred_element_type=F32)
-        old = mo[rb * HEADS + h]
+        old = mo[i]
         top = jnp.maximum(jnp.max(sa, axis=1, keepdims=True) * SCALE, old)
         acc = jnp.dot(jnp.exp2(sa * SCALE - top[:, 0:1]).astype(BF), ava[...], preferred_element_type=F32)
         keep = jnp.exp2(old - top)
-        acc = acc + acco[rb * HEADS + h] * jnp.concatenate([keep, keep], axis=1)
+        acc = acc + acco[i] * jnp.concatenate([keep, keep], axis=1)
         obuf[rows, cols] = (acc[:, :HD] / acc[:, HD:]).astype(BF)
 
     stores = [
@@ -342,27 +360,12 @@
         for rb in range(NRB)
     ]
 
-    def anchor_steps(rb):
-        @pl.loop(0, HEADS // HG)
+    def anchor_steps(start, steps):
+        @pl.loop(0, 2)
         def _(i):
-            for u in range(HG):
-                anchor_step(rb, i * HG + u)
-
-        stores[rb].start()
-
-    for d in range(1, NY):
-        recv(akv.at[at_c(-d), :, data], S_AD + d - 1)
-    alen = akv[c, z, SL:SL + 16, :].astype(F32)
-    alive_to = jnp.where(ctx == 0, 0.0, alen[0:1] * 128.0 + alen[8:9])
-    anchor = akv[:, :, 0:SL, :].reshape(2 * ROWS, HD)
-    for a in range(3):
-        keys_at = a * THIRD
-        live_keys(
-            (row_of + a * THIRD).astype(F32) < alive_to, anchor[keys_at:keys_at + THIRD], anchor[0:1],
-            anchor[ROWS + keys_at:ROWS + keys_at + THIRD], akk, ava, slice(a * THIRD, (a + 1) * THIRD),
-        )
-
-    anchor_steps(0)
+            for u in range(steps // 2):
+                anchor_step(start + i * (steps // 2) + u)
+
     load_w.wait()
     for k in range(NZ):
         for d in range(1, NY):
@@ -376,7 +379,23 @@
     psend[...] = partial.astype(BF)
     for d in range(1, TP):
         send(psend.at[at_t(d)], prec.at[t], S_RX + d - 1, dev(c, z, at_t(d)))
-    anchor_steps(1)
+    for d in range(1, NY):
+        recv(akv.at[at_c(-d), :, data], S_AD + d - 1)
+    alen = akv[c, z, SL:SL + 16, :].astype(F32)
+    alive_to = jnp.where(ctx == 0, 0.0, alen[0:1] * 128.0 + alen[8:9])
+    anchor_k, anchor_v = (
+        jnp.concatenate([akv[(p + 2) % 4, n:n + 4, 0:SL, :].reshape(4 * SL, HD) for p in range(4)], axis=0)
+        for n in (0, 4)
+    )
+    for a in range(3):
+        part = slice(a * THIRD, (a + 1) * THIRD)
+        live_keys(
+            (row_of + a * THIRD).astype(F32) < alive_to, anchor_k[part], anchor_k[0:1], anchor_v[part],
+            akk, ava, part,
+        )
+
+    anchor_steps(0, 14)
+    stores[0].start()
     for d in range(1, TP):
         recv(prec.at[at_t(-d)], S_RX + d - 1)
     answer = pown[t]
@@ -385,7 +404,9 @@
     ansb[t] = answer.astype(BF)
     for d in range(1, TP):
         send(ansb.at[t], ansb.at[t], S_GX + d - 1, dev(c, z, at_t(d)))
-    anchor_steps(2)
+    anchor_steps(14, 10)
+    stores[1].start()
+    stores[2].start()
     for d in range(1, TP):
         recv(ansb.at[at_t(-d)], S_GX + d - 1)
     ans[...] = ansb[...].reshape(ans.shape)
@@ -453,15 +474,15 @@
             v((NRB * HEADS, TILE, 2 * HD), F32),
             v(cq.shape, BF),
             v((NZ, 80, HD), BF),
-            v((NY, 48, HD), BF),
+            v((NY + 1, 48, HD), BF),
             v((NZ, SL + 16, HD), BF),
             v((4, NZ, SL + 16, HD), BF),
             v((2 * ROWS, HD), BF),
             v((2 * ROWS, 2 * HD), BF),
             v((NZ * 64, HD), F32),
             v((NZ * 64, 2 * HD), F32),
-            v((NZ, 96, HD), BF),
-            v((NZ, 96, HD), BF),
+            v((NZ, 80, HD), BF),
+            v((NZ, 80, HD), BF),
             v((NY, NZ, 16, 4 * HD), BF),
             v((TP, NY * NZ, columns), F32),
             v((TP, NY * NZ, columns), BF),

time: 64.1 us -> 62.3 us (0.972)
  Pallas kernels: 62.5 us -> 60.7 us
    pallas_call x1, Pallas kernels: 60.3 us -> 58.5 us  [body(): pl.pallas_call(kernel, out_shape=(jax.ShapeDtypeStruct(cq.shape, BF), jax...]
where the time goes in v6:
time: 62.3 us; the launch traced here: 62.2 us
  Pallas kernels  60.7 us (97%)
  between operations  1.45 us (2%)
    pallas_call x1, Pallas kernels, body(): pl.pallas_call(kernel, out_shape=(jax.ShapeDtypeStruct(cq.shape, BF), jax...  58.5 us
    pallas_call x1, Pallas kernels, body(): pl.pallas_call(finish, out_shape=tuple((jax.ShapeDtypeStruct(x.shape, x.d...  2.26 us

profile of v6, /device:TPU:1, one launch (start us, length us, event | category | flops | bytes accessed | tf_op | source)
XLA Modules:
  0.0 62.2 jit_solution(15063719417938237431)
XLA Ops:
  1.3 58.5 %star_attention.1 = (bf16[768,1024]{1,0:T(8,128)(2,1)}, bf16[256,256]{1,0:T(8,128)(2,1)}) custom-call(bf16[768,1024]{1,0:T(8,128)(2,1)} %cq.1, bf16[768,128]{1,0:T(8,128)(2,1)} %ck.1, bf16[768,128]{1,0:T(8,128)(2,1)} %cv.1, s32[1]{0:T(128)S(6)} %copy.11.blen, bf16[8,1024]{1,0:T(8,128)(2,1)} %qq_hbm.1, bf16[8,128]{1,0:T(8,128)(2,1)} %qk_hbm.1, ...), custom_call_target="tpu_custom_call" | custom-call | tf_op jit(solution)/shard_map/star_attention/pallas_call | solution.py:453
  59.7 2.3 %results.1 = (bf16[768,1024]{1,0:T(8,128)(2,1)}, bf16[256,256]{1,0:T(8,128)(2,1)}) custom-call(bf16[768,1024]{1,0:T(8,128)(2,1)} %get-tuple-element.4.block, bf16[256,256]{1,0:T(8,128)(2,1)} %get-tuple-element.5.answer), custom_call_target="tpu_custom_call" | custom-call | tf_op jit(solution)/shard_map/results/pallas_call | solution.py:500

commit v7 on v6

--- a/solution.py
+++ b/solution.py
@@ -149,7 +149,6 @@
     for d in YORDER:
         send(sml.at[c], sml.at[c], S_SM + d - 1, next_to(d))
     send(sml.at[c], sml.at[NY], S_SM + 3, dev(at_c(2), at_z(1), t))
-    send_keys(1)
     for copy in loads:
         copy.wait()
 
@@ -196,6 +195,7 @@
     own_steps(0)
 
     own_steps(1)
+    send_keys(1)
     own_steps(2)
 
     for d in range(1, NZ):
@@ -366,19 +366,6 @@
             for u in range(steps // 2):
                 anchor_step(start + i * (steps // 2) + u)
 
-    load_w.wait()
-    for k in range(NZ):
-        for d in range(1, NY):
-            recv(abuf.at[at_c(-d), lax.rem(z_from(d) - k + NZ, NZ)], S_TY + 3 * k + d - 1)
-
-    rows = jnp.concatenate([abuf[(yy + 2 * zz) % NY, zz] for yy in range(NY) for zz in range(NZ)], axis=0)
-    upper = jnp.dot(rows, wv[0:4 * HD], preferred_element_type=F32).reshape(NY * NZ, 16, -1)
-    lower = jnp.dot(rows, wv[4 * HD:], preferred_element_type=F32).reshape(NY * NZ, 16, -1)
-    partial = (upper[:, 0:8] + lower[:, 8:16]).reshape(pown.shape)
-    pown[...] = partial
-    psend[...] = partial.astype(BF)
-    for d in range(1, TP):
-        send(psend.at[at_t(d)], prec.at[t], S_RX + d - 1, dev(c, z, at_t(d)))
     for d in range(1, NY):
         recv(akv.at[at_c(-d), :, data], S_AD + d - 1)
     alen = akv[c, z, SL:SL + 16, :].astype(F32)
@@ -394,8 +381,23 @@
             akk, ava, part,
         )
 
-    anchor_steps(0, 14)
+    anchor_steps(0, 4)
+    load_w.wait()
+    for k in range(NZ):
+        for d in range(1, NY):
+            recv(abuf.at[at_c(-d), lax.rem(z_from(d) - k + NZ, NZ)], S_TY + 3 * k + d - 1)
+
+    rows = jnp.concatenate([abuf[(yy + 2 * zz) % NY, zz] for yy in range(NY) for zz in range(NZ)], axis=0)
+    upper = jnp.dot(rows, wv[0:4 * HD], preferred_element_type=F32).reshape(NY * NZ, 16, -1)
+    lower = jnp.dot(rows, wv[4 * HD:], preferred_element_type=F32).reshape(NY * NZ, 16, -1)
+    partial = (upper[:, 0:8] + lower[:, 8:16]).reshape(pown.shape)
+    pown[...] = partial
+    psend[...] = partial.astype(BF)
+    for d in range(1, TP):
+        send(psend.at[at_t(d)], prec.at[t], S_RX + d - 1, dev(c, z, at_t(d)))
+    anchor_steps(4, 12)
     stores[0].start()
+    stores[1].start()
     for d in range(1, TP):
         recv(prec.at[at_t(-d)], S_RX + d - 1)
     answer = pown[t]
@@ -404,8 +406,7 @@
     ansb[t] = answer.astype(BF)
     for d in range(1, TP):
         send(ansb.at[t], ansb.at[t], S_GX + d - 1, dev(c, z, at_t(d)))
-    anchor_steps(14, 10)
-    stores[1].start()
+    anchor_steps(16, 8)
     stores[2].start()
     for d in range(1, TP):
         recv(ansb.at[at_t(-d)], S_GX + d - 1)

time: 62.3 us -> 61.8 us (level)
  no operation moved by 1% of the time
where the time goes in v7:
time: 61.8 us; the launch traced here: 61.7 us
  Pallas kernels  60.2 us (97%)
  between operations  1.45 us (2%)
    pallas_call x1, Pallas kernels, body(): pl.pallas_call(kernel, out_shape=(jax.ShapeDtypeStruct(cq.shape, BF), jax...  58 us
    pallas_call x1, Pallas kernels, body(): pl.pallas_call(finish, out_shape=tuple((jax.ShapeDtypeStruct(x.shape, x.d...  2.26 us

profile of v7, /device:TPU:1, one launch (start us, length us, event | category | flops | bytes accessed | tf_op | source)
XLA Modules:
  0.0 61.7 jit_solution(16413560340981845978)
XLA Ops:
  1.3 58.0 %star_attention.1 = (bf16[768,1024]{1,0:T(8,128)(2,1)}, bf16[256,256]{1,0:T(8,128)(2,1)}) custom-call(bf16[768,1024]{1,0:T(8,128)(2,1)} %cq.1, bf16[768,128]{1,0:T(8,128)(2,1)} %ck.1, bf16[768,128]{1,0:T(8,128)(2,1)} %cv.1, s32[1]{0:T(128)S(6)} %copy.11.blen, bf16[8,1024]{1,0:T(8,128)(2,1)} %qq_hbm.1, bf16[8,128]{1,0:T(8,128)(2,1)} %qk_hbm.1, ...), custom_call_target="tpu_custom_call" | custom-call | tf_op jit(solution)/shard_map/star_attention/pallas_call | solution.py:454
  59.2 2.3 %results.1 = (bf16[768,1024]{1,0:T(8,128)(2,1)}, bf16[256,256]{1,0:T(8,128)(2,1)}) custom-call(bf16[768,1024]{1,0:T(8,128)(2,1)} %get-tuple-element.4.block, bf16[256,256]{1,0:T(8,128)(2,1)} %get-tuple-element.5.answer), custom_call_target="tpu_custom_call" | custom-call | tf_op jit(solution)/shard_map/results/pallas_call | solution.py:501

commit v8 on v7

--- a/solution.py
+++ b/solution.py
@@ -24,7 +24,9 @@
 THIRD = ROWS // 3
 SCALE = math.log2(math.e) / math.sqrt(HD)
 LOG2E = math.log2(math.e)
-ZORDER = (1, 7, 2, 6, 3, 5, 4)
+ZORDER = (3, 5, 4, 1, 7, 2, 6)
+TORDER = (4, 3, 5, 2, 6, 1, 7)
+ARRIVAL = (2, 6, 1, 7, 4, 3, 5)
 YORDER = (1, 3, 2)
 COPIES = 4
 HG = 4
@@ -341,7 +343,7 @@
     for d in YORDER:
         send(akv.at[c, :, data], akv.at[c, :, data], S_AD + d - 1, next_to(d))
 
-    for k in ZORDER:
+    for k in ARRIVAL:
         pass_on(k)
 
     def anchor_step(i):
@@ -393,7 +395,7 @@
     partial = (upper[:, 0:8] + lower[:, 8:16]).reshape(pown.shape)
     pown[...] = partial
     psend[...] = partial.astype(BF)
-    for d in range(1, TP):
+    for d in TORDER:
         send(psend.at[at_t(d)], prec.at[t], S_RX + d - 1, dev(c, z, at_t(d)))
     anchor_steps(4, 12)
     stores[0].start()
@@ -404,7 +406,7 @@
     for d in range(1, TP):
         answer = answer + prec[at_t(-d)].astype(F32)
     ansb[t] = answer.astype(BF)
-    for d in range(1, TP):
+    for d in TORDER:
         send(ansb.at[t], ansb.at[t], S_GX + d - 1, dev(c, z, at_t(d)))
     anchor_steps(16, 8)
     stores[2].start()

time: 61.8 us -> 60.2 us (0.974)
  Pallas kernels: 60.2 us -> 58.7 us
    pallas_call x1, Pallas kernels: 58 us -> 56.4 us  [body(): pl.pallas_call(kernel, out_shape=(jax.ShapeDtypeStruct(cq.shape, BF), jax...]
where the time goes in v8:
time: 60.2 us; the launch traced here: 60.1 us
  Pallas kernels  58.7 us (98%)
  between operations  1.45 us (2%)
    pallas_call x1, Pallas kernels, body(): pl.pallas_call(kernel, out_shape=(jax.ShapeDtypeStruct(cq.shape, BF), jax...  56.4 us
    pallas_call x1, Pallas kernels, body(): pl.pallas_call(finish, out_shape=tuple((jax.ShapeDtypeStruct(x.shape, x.d...  2.26 us

profile of v8, /device:TPU:1, one launch (start us, length us, event | category | flops | bytes accessed | tf_op | source)
XLA Modules:
  0.0 60.1 jit_solution(4808246301175889412)
XLA Ops:
  1.3 56.4 %star_attention.1 = (bf16[768,1024]{1,0:T(8,128)(2,1)}, bf16[256,256]{1,0:T(8,128)(2,1)}) custom-call(bf16[768,1024]{1,0:T(8,128)(2,1)} %cq.1, bf16[768,128]{1,0:T(8,128)(2,1)} %ck.1, bf16[768,128]{1,0:T(8,128)(2,1)} %cv.1, s32[1]{0:T(128)S(6)} %copy.11.blen, bf16[8,1024]{1,0:T(8,128)(2,1)} %qq_hbm.1, bf16[8,128]{1,0:T(8,128)(2,1)} %qk_hbm.1, ...), custom_call_target="tpu_custom_call" | custom-call | tf_op jit(solution)/shard_map/star_attention/pallas_call | solution.py:456
  57.7 2.3 %results.1 = (bf16[768,1024]{1,0:T(8,128)(2,1)}, bf16[256,256]{1,0:T(8,128)(2,1)}) custom-call(bf16[768,1024]{1,0:T(8,128)(2,1)} %get-tuple-element.4.block, bf16[256,256]{1,0:T(8,128)(2,1)} %get-tuple-element.5.answer), custom_call_target="tpu_custom_call" | custom-call | tf_op jit(solution)/shard_map/results/pallas_call | solution.py:503

commit v9 on v8

--- a/solution.py
+++ b/solution.py
@@ -284,21 +284,25 @@
 
     phase_two((2,))
 
-    total = acc2[:, HD:]
-    lse = m2[...] + jnp.log(total) * LOG2E
-    part_out = acc2[:, :HD] / total
-    for j in range(NZ):
+    def pack(j):
+        at = pl.ds(pl.multiple_of(j * 64, 64), 64)
+        acc = acc2[at, :]
+        total = acc[:, HD:]
+        lse = m2[at, :] + jnp.log(total) * LOG2E
         compact = jnp.zeros((8, HD), F32)
         for h in range(HEADS):
-            compact = jnp.where(lane8 == h, lse[j * 64 + h * 8:j * 64 + h * 8 + 8], compact)
+            compact = jnp.where(lane8 == h, lse[h * 8:h * 8 + 8], compact)
         high = compact.astype(BF).astype(F32)
         middle = (compact - high).astype(BF).astype(F32)
         low = compact - high - middle
-        cmsg[j, 0:64, :] = part_out[j * 64:(j + 1) * 64].astype(BF)
+        cmsg[j, 0:64, :] = (acc[:, :HD] / total).astype(BF)
         pieces = high + pltpu.roll(middle, 8, 1) + pltpu.roll(low, 16, 1)
         cmsg[j, 64:80, :] = jnp.concatenate([pieces, pieces], axis=0).astype(BF)
+
     for d in ZORDER:
+        pack(at_z(d))
         send(cmsg.at[at_z(d)], crecv.at[z], S_PZ + d - 1, dev(c, at_z(d), t))
+    pack(z)
 
     @pl.when(z != source_z)
     def _():

time: 60.2 us -> 60.3 us (level)
  no operation moved by 1% of the time
where the time goes in v9:
time: 60.3 us; the launch traced here: 60.1 us
  Pallas kernels  58.7 us (97%)
  between operations  1.45 us (2%)
    pallas_call x1, Pallas kernels, body(): pl.pallas_call(kernel, out_shape=(jax.ShapeDtypeStruct(cq.shape, BF), jax...  56.4 us
    pallas_call x1, Pallas kernels, body(): pl.pallas_call(finish, out_shape=tuple((jax.ShapeDtypeStruct(x.shape, x.d...  2.26 us

profile of v9, /device:TPU:1, one launch (start us, length us, event | category | flops | bytes accessed | tf_op | source)
XLA Modules:
  0.0 60.1 jit_solution(98424208746988774)
XLA Ops:
  1.3 56.4 %star_attention.1 = (bf16[768,1024]{1,0:T(8,128)(2,1)}, bf16[256,256]{1,0:T(8,128)(2,1)}) custom-call(bf16[768,1024]{1,0:T(8,128)(2,1)} %cq.1, bf16[768,128]{1,0:T(8,128)(2,1)} %ck.1, bf16[768,128]{1,0:T(8,128)(2,1)} %cv.1, s32[1]{0:T(128)S(6)} %copy.11.blen, bf16[8,1024]{1,0:T(8,128)(2,1)} %qq_hbm.1, bf16[8,128]{1,0:T(8,128)(2,1)} %qk_hbm.1, ...), custom_call_target="tpu_custom_call" | custom-call | tf_op jit(solution)/shard_map/star_attention/pallas_call | solution.py:460
  57.7 2.3 %results.1 = (bf16[768,1024]{1,0:T(8,128)(2,1)}, bf16[256,256]{1,0:T(8,128)(2,1)}) custom-call(bf16[768,1024]{1,0:T(8,128)(2,1)} %get-tuple-element.4.block, bf16[256,256]{1,0:T(8,128)(2,1)} %get-tuple-element.5.answer), custom_call_target="tpu_custom_call" | custom-call | tf_op jit(solution)/shard_map/results/pallas_call | solution.py:507
